TPU v7x, 256 devices: a whole 4x4x8 slice. The times are simulated.
256 devices in a mesh: edge: 32 (over z, x), bucket: 8 (over y, core).
Axes of the slice: x: 4, y: 4, z: 8, core: 2. Of those that a mesh axis runs over, the one named last changes fastest.
Arguments:
- unit_cost: float32 [256, 131072], P('bucket', 'edge'), may hold values from 0.2 to 2
- upper_bound: float32 [256, 131072], P('bucket', 'edge'), may hold values from 0.5 to 4
- start_primal: float32 [256, 131072], P('bucket', 'edge'), may hold values from 0 to 2
- start_dual: float32 [256, 8192], P('bucket', 'edge'), may hold values from -6 to 6
- net_target: float32 [256, 8192], P('bucket', 'edge'), may hold values from -12 to 12
- owners: int32 [131072, 2], P('edge'), may hold values from 0 to 31, all different within a row; in each aligned block of 4096 rows (0 to 4095, 4096 to 8191, ...) at most 512 rows name the same one
- local_ids: int32 [131072, 2], P('edge'), may hold values from 0 to 255
Outputs:
- primal: float32 [256, 131072], P('bucket', 'edge')
- duals: float32 [256, 8192], P('bucket', 'edge')
- totals: float32 [2, 3, 256], P(None, None, 'bucket')
Inputs may be any that keep to these rules, and one draw needn't show every extreme that they name: The two owners of an edge differ. Of the edges of one index of edge, at most 512 name any one owner, and in every draw some owner is named by exactly 512 of them.
All inputs are finite; a program needn't handle non-finite values.
Results may differ from a plain program's by a relative error of at most 0.0001.
Values sent between devices are 32-bit elements; how exact they have to be, the bound alone decides.
A program may use at most 128 MiB of HBM per device.

v0:
```python
import jax
import jax.numpy as jnp
from jax import lax
from jax.sharding import PartitionSpec as P

ITERS = 3


def body(unit_cost, upper_bound, start_primal, start_dual, net_target, owners, local_ids):
    edges_here = unit_cost.shape[1]
    accounts_here = start_dual.shape[1]
    parties = lax.axis_size("edge")
    holder = owners.T.reshape(-1)
    within = local_ids.T.reshape(-1)
    global_ids = holder * accounts_here + within
    duals, target = (start_dual, net_target)

    def to_owners(pushed):
        partial_value = (
            jnp.zeros((pushed.shape[0], accounts_here * parties), jnp.float32)
            .at[:, global_ids]
            .add(pushed)
        )
        return lax.psum_scatter(partial_value, "edge", scatter_dimension=1, tiled=True)

    unit_terms = jnp.ones((1, 2 * edges_here), jnp.float32)
    degree = to_owners(unit_terms)
    dual_step = 1.0 / jnp.maximum(degree, 1.0)
    primal = start_primal
    squares, spends = ([], [])
    for sweep in range(ITERS):
        gathered = lax.all_gather(duals, "edge", axis=1, tiled=True)
        values = jnp.take(gathered, global_ids, axis=1)
        pulled = values[:, :edges_here] - values[:, edges_here:]
        moved = jnp.clip(primal - 0.5 * (unit_cost - pulled), 0.0, upper_bound)
        extended = 2.0 * moved - primal
        applied = to_owners(jnp.concatenate([extended, -extended], axis=1))
        residual = target - applied
        duals = duals + dual_step * residual
        primal = moved
        square_here = jnp.sum(residual * residual, axis=1)
        spend_here = jnp.sum(unit_cost * moved, axis=1)
        square_all, spend_all = lax.psum((square_here, spend_here), "edge")
        squares.append(square_all)
        spends.append(spend_all)
    totals = jnp.stack([jnp.stack(squares), jnp.stack(spends)])
    return (primal, duals, totals)


def solution(mesh):
    return jax.shard_map(
        body,
        mesh=mesh,
        in_specs=(
            P("bucket", "edge"),
            P("bucket", "edge"),
            P("bucket", "edge"),
            P("bucket", "edge"),
            P("bucket", "edge"),
            P("edge", None),
            P("edge", None),
        ),
        out_specs=(P("bucket", "edge"), P("bucket", "edge"), P(None, None, "bucket")),
        check_vma=False,
    )
```

profile of v0, /device:TPU:16, one launch (start us, length us, event | category | flops | bytes accessed | tf_op | source)
XLA Modules:
  0.0 1390.6 jit_solution(8145512875284047542)
XLA Ops:
  7.2 1.5 copy.57
  8.8 0.8 fusion.25
  9.7 43.2 %scatter_custom_fusion = f32[8192]{0:T(1024)S(1)} fusion(s32[8192]{0:T(1024)S(1)} %bitcast.43, f32[8192]{0:T(1024)S(1)} %broadcast.58, f32[]{:T(128)} %constant.15.clone.1), kind=kCustom, calls=%fused_computation.55 | custom fusion | flops 8192 | bytes 32772 | tf_op jit(solution)/shard_map/scatter-add | solution.py:22
  52.9 2.6 copy.70
  55.7 40.1 %all-gather.4.cloned.1.call-done = f32[32,8192]{0,1:T(8,128)} async-done(((f32[32,256]{0,1:T(8,128)}), f32[32,8192]{0,1:T(8,128)}) %all-gather.4.cloned.1.call-update) | async-done | bytes 1048592 | tf_op jit(solution)/shard_map/all_gather | solution.py:32
  95.8 29.9 %gather_fusion = f32[8192,32]{1,0:T(8,128)} fusion(f32[32,8192]{0,1:T(8,128)} %all-gather.4.cloned.1.call-done, s32[8192]{0:T(1024)S(1)} %fusion.21), kind=kCustom, calls=%fused_computation.clone | custom fusion | bytes 2129920 | tf_op jit(solution)/shard_map/jit(_take)/gather | solution.py:33
  125.7 2.9 copy.58
  128.7 0.3 fusion.30
  129.1 2.7 copy.59
  131.8 46.5 %scatter_custom_fusion.1 = f32[32,8192]{0,1:T(8,128)} fusion(s32[8192]{0:T(1024)S(1)} %bitcast.44, f32[8192,32]{1,0:T(8,128)} %copy.59, f32[]{:T(128)} %constant.15.clone.1), kind=kCustom, calls=%fused_computation.11 | custom fusion | flops 262144 | bytes 1049088 | tf_op jit(solution)/shard_map/scatter-add | solution.py:22
  178.4 139.7 %reduce-scatter.13.cloned.1.call-done = f32[256,1]{1,0:T(8,128)} async-done(((f32[8192,1]{1,0:T(8,128)}), f32[256,1]{1,0:T(8,128)}) %reduce-scatter.13.cloned.1.call-update) | async-done | bytes 1040
  318.2 0.9 divide_bitcast_fusion
  319.2 222.8 %reduce-scatter.7.cloned.1.call-done = f32[32,256]{0,1:T(8,128)} async-done(((f32[32,8192]{0,1:T(8,128)}), f32[32,256]{0,1:T(8,128)}) %reduce-scatter.7.cloned.1.call-update) | async-done | bytes 32784 | tf_op jit(solution)/shard_map/reduce_scatter | solution.py:24
  541.9 1.7 multiply_add_fusion.2
  543.7 81.3 %all-gather.6.cloned.1.call-done = f32[32,8192]{0,1:T(8,128)} async-done(((f32[32,256]{0,1:T(8,128)}), f32[32,8192]{0,1:T(8,128)}) %all-gather.6.cloned.1.call-update) | async-done | bytes 1048592 | tf_op jit(solution)/shard_map/all_gather | solution.py:32
  624.9 29.9 %gather_fusion.1 = f32[8192,32]{1,0:T(8,128)} fusion(f32[32,8192]{0,1:T(8,128)} %all-gather.6.cloned.1.call-done, s32[8192]{0:T(1024)S(1)} %fusion.21), kind=kCustom, calls=%fused_computation.1.clone | custom fusion | bytes 2129920 | tf_op jit(solution)/shard_map/jit(_take)/gather | solution.py:33
  654.8 2.8 copy.62
  658.1 2.7 copy.63
  660.8 46.5 %scatter_custom_fusion.2 = f32[32,8192]{0,1:T(8,128)} fusion(s32[8192]{0:T(1024)S(1)} %bitcast.45, f32[8192,32]{1,0:T(8,128)} %copy.63, f32[]{:T(128)} %constant.15.clone.1), kind=kCustom, calls=%fused_computation.9 | custom fusion | flops 262144 | bytes 1049088 | tf_op jit(solution)/shard_map/scatter-add | solution.py:22
  707.3 218.4 %reduce-scatter.9.cloned.1.call-done = f32[32,256]{0,1:T(8,128)} async-done(((f32[32,8192]{0,1:T(8,128)}), f32[32,256]{0,1:T(8,128)}) %reduce-scatter.9.cloned.1.call-update) | async-done | bytes 32784 | tf_op jit(solution)/shard_map/reduce_scatter | solution.py:24
  925.7 1.7 multiply_add_fusion.1
  927.6 80.9 %all-gather.8.cloned.1.call-done = f32[32,8192]{0,1:T(8,128)} async-done(((f32[32,256]{0,1:T(8,128)}), f32[32,8192]{0,1:T(8,128)}) %all-gather.8.cloned.1.call-update) | async-done | bytes 1048592 | tf_op jit(solution)/shard_map/all_gather | solution.py:32
  1008.4 29.9 %gather_fusion.2 = f32[8192,32]{1,0:T(8,128)} fusion(f32[32,8192]{0,1:T(8,128)} %all-gather.8.cloned.1.call-done, s32[8192]{0:T(1024)S(1)} %fusion.21), kind=kCustom, calls=%fused_computation.2.clone | custom fusion | bytes 2129920 | tf_op jit(solution)/shard_map/jit(_take)/gather | solution.py:33
  1038.3 2.8 copy.65
  1041.2 0.4 multiply_reduce_fusion.2
  1041.8 2.7 copy.66
  1044.5 46.5 %scatter_custom_fusion.3 = f32[32,8192]{0,1:T(8,128)} fusion(s32[8192]{0:T(1024)S(1)} %bitcast.46, f32[8192,32]{1,0:T(8,128)} %copy.66, f32[]{:T(128)} %constant.15.clone.1), kind=kCustom, calls=%fused_computation.7 | custom fusion | flops 262144 | bytes 1049088 | tf_op jit(solution)/shard_map/scatter-add | solution.py:22
  1091.0 218.3 %reduce-scatter.11.cloned.1.call-done = f32[32,256]{0,1:T(8,128)} async-done(((f32[32,8192]{0,1:T(8,128)}), f32[32,256]{0,1:T(8,128)}) %reduce-scatter.11.cloned.1.call-update) | async-done | bytes 32784 | tf_op jit(solution)/shard_map/reduce_scatter | solution.py:24
  1309.3 1.0 multiply_reduce_fusion.5
  1310.3 72.2 %all-reduce = (f32[1,32]{1,0:T(1,128)S(1)}, f32[1,32]{1,0:T(1,128)S(1)}, f32[1,32]{1,0:T(1,128)S(1)}, f32[1,32]{1,0:T(1,128)S(1)}, f32[1,32]{1,0:T(1,128)S(1)}, /*index=5*/f32[1,32]{1,0:T(1,128)S(1)}) all-reduce(f32[1,32]{1,0:T(1,128)S(1)} %bitcast.51, f32[1,32]{1,0:T(1,128)S(1)} %bitcast.52, ...), channel_id=1, replica_groups=mesh['edge'=32,'bucket'=8] {'edge'}, use_global_device_ids=true, to_apply=%region_19.21 | all-reduce | flops 192 | bytes 1536 | tf_op jit(solution)/shard_map/psum | solution.py:43
  1382.5 0.6 copy.69
  1383.1 0.7 copy.68
  (52 shorter events, 1.7 us)
Async XLA Ops:
  7.2 88.6 %all-gather.4.cloned.1.call-start = ((), (), s32[]{:S(2)}) async-start(), calls=%async_computation.4 | async-start | bytes 4325376 | tf_op jit(solution)/shard_map/all_gather | solution.py:32
  8.7 309.4 %reduce-scatter.13.cloned.1.call-start = ((), (), s32[]{:S(2)}) async-start(), calls=%async_computation.10 | async-start | bytes 4325376
  55.6 486.4 %reduce-scatter.7.cloned.1.call-start = ((), (), s32[]{:S(2)}) async-start(), calls=%async_computation.5 | async-start | bytes 4325376 | tf_op jit(solution)/shard_map/reduce_scatter | solution.py:24
  125.7 3.0 copy-start
  125.7 3.0 copy-start.1
  125.7 3.1 copy-start.8
  131.8 46.6 %copy-start.9 = (f32[32,256]{1,0:T(8,128)S(1)}, f32[32,256]{1,0:T(8,128)}, u32[]{:S(2)}) copy-start(f32[32,256]{1,0:T(8,128)} %param.13) | copy-start | bytes 98308
  131.8 410.2 %copy-start.3 = (f32[32,256]{0,1:T(8,128)S(1)}, f32[32,256]{0,1:T(8,128)}, u32[]{:S(2)}) copy-start(f32[32,256]{0,1:T(8,128)} %copy.57) | copy-start | bytes 98308
  178.3 446.7 %all-gather.6.cloned.1.call-start = ((), (), s32[]{:S(2)}) async-start(), calls=%async_computation.6 | async-start | bytes 4325376 | tf_op jit(solution)/shard_map/all_gather | solution.py:32
  543.6 382.0 %reduce-scatter.9.cloned.1.call-start = ((), (), s32[]{:S(2)}) async-start(), calls=%async_computation.7 | async-start | bytes 4325376 | tf_op jit(solution)/shard_map/reduce_scatter | solution.py:24
  660.7 264.9 %copy-start.5 = (f32[32,256]{0,1:T(8,128)S(1)}, f32[32,256]{0,1:T(8,128)}, u32[]{:S(2)}) copy-start(f32[32,256]{0,1:T(8,128)} %multiply_add_fusion.2) | copy-start | bytes 98308
  707.2 301.2 %all-gather.8.cloned.1.call-start = ((), (), s32[]{:S(2)}) async-start(), calls=%async_computation.8 | async-start | bytes 4325376 | tf_op jit(solution)/shard_map/all_gather | solution.py:32
  927.3 382.0 %reduce-scatter.11.cloned.1.call-start = ((), (), s32[]{:S(2)}) async-start(), calls=%async_computation.9 | async-start | bytes 4325376 | tf_op jit(solution)/shard_map/reduce_scatter | solution.py:24
  1041.6 2.8 copy-start.2
  1044.5 264.8 %copy-start.4 = (f32[32,256]{0,1:T(8,128)S(1)}, f32[32,256]{0,1:T(8,128)}, u32[]{:S(2)}) copy-start(f32[32,256]{0,1:T(8,128)} %multiply_add_fusion.1) | copy-start | bytes 98308
  1044.5 264.8 %copy-start.6 = (f32[32,256]{0,1:T(8,128)S(1)}, f32[32,256]{0,1:T(8,128)}, u32[]{:S(2)}) copy-start(f32[32,256]{0,1:T(8,128)} %reduce-scatter.7.cloned.1.call-done) | copy-start | bytes 98308
  1044.5 264.8 %copy-start.7 = (f32[32,256]{0,1:T(8,128)S(1)}, f32[32,256]{0,1:T(8,128)}, u32[]{:S(2)}) copy-start(f32[32,256]{0,1:T(8,128)} %reduce-scatter.9.cloned.1.call-done) | copy-start | bytes 98308
Sparse Core Ops, SparseCore 0:
  11.2 84.5 all-gather.3
  99.6 218.4 reduce-scatter.12
  322.6 219.3 reduce-scatter.6
  544.9 79.9 all-gather.5
  707.3 218.2 reduce-scatter.8
  928.4 79.9 all-gather.7
  1091.1 218.1 reduce-scatter.10
where the time goes:
time: 1390 us
  waiting for transfers between devices  1000 us (72%)
  other arithmetic  190 us (14%)
  local copies, waits for them, and re-layouts  112 us (8%)
  blocking collectives  72.2 us (5%)
  between operations  14.3 us (1%)
    reduce_scatter x3, waiting for transfers between devices, to_owners(): lax.psum_scatter(partial_value, 'edge', scatter_dimension=1, tiled=True)  659 us
    all_gather x3, waiting for transfers between devices, body(): gathered = lax.all_gather(duals, 'edge', axis=1, tiled=True)  202 us
    scatter-add x4, other arithmetic, to_owners(): partial_value = jnp.zeros((pushed.shape[0], accounts_here * parties), jnp...  183 us
    unnamed x8, waiting for transfers between devices  140 us
    gather x6, local copies, waits for them, and re-layouts, body(): values = jnp.take(gathered, global_ids, axis=1)  98.2 us
    psum x1, blocking collectives, body(): square_all, spend_all = lax.psum((square_here, spend_here), 'edge')  72.2 us
  transfers between devices with their start and end apart: 7, of which 7 were waited for; matrix products, arithmetic and copies ran while one was open for 9% of the time, Pallas kernels for 0%

commit v1 on v0

v1 whole, which is shorter than its diff:
```python
import functools

import jax
import jax.numpy as jnp
from jax import lax
from jax.experimental import pallas as pl
from jax.experimental.pallas import tpu as pltpu
from jax.sharding import PartitionSpec as P

ITERS = 3
X = 4
Z = 8
CH = 8
PULL = 2048
PUSH = 4096
F32 = jnp.float32
BF16 = jnp.bfloat16


def split(value):
    high = value.astype(BF16)
    low = (value - high.astype(F32)).astype(BF16)
    return high, low


def kernel(cost_ref, bound_ref, start_ref, dual_ref, target_ref, owner_ref, local_ref,
           primal_ref, duals_ref, totals_ref,
           hot, hot_t, own_row, own_half, ext, gath, part, rsx, zsum, rsz,
           deg_part, deg_x, deg_z, step_ref, spend_ref, tot, tot_z, tot_x,
           sem_agz, sem_agx, sem_rsx, sem_rsz, sem_dx, sem_dz, sem_tz, sem_tx):
    edges = cost_ref.shape[1]
    chunks = cost_ref.shape[0] // CH
    slots = ITERS * chunks
    me = lax.axis_index("edge")
    my_x = lax.rem(me, X)
    my_z = lax.div(me, X)

    def at_x(j):
        return my_z * X + lax.rem(my_x + j, X)

    def at_z(j):
        return lax.rem(my_z + j, Z) * X + my_x

    def remote(src, dst, sems, device):
        return pltpu.make_async_remote_copy(
            src_ref=src, dst_ref=dst, send_sem=sems.at[0], recv_sem=sems.at[1],
            device_id={"edge": device}, device_id_type=pl.DeviceIdType.MESH)

    def agz(c):
        block = gath.at[c, my_x, my_z]
        return [remote(block, block, sem_agz.at[c, j - 1], at_z(j)) for j in range(1, Z)]

    def agx(c):
        block = gath.at[c, my_x]
        return [remote(block, block, sem_agx.at[c, j - 1], at_x(j)) for j in range(1, X)]

    def to_x(c):
        return [remote(part.at[c, lax.rem(my_x + j, X)], rsx.at[c, j - 1], sem_rsx.at[c, j - 1], at_x(j))
                for j in range(1, X)]

    def to_z(c):
        return [remote(zsum.at[c, lax.rem(my_z + j, Z)], rsz.at[c, j - 1], sem_rsz.at[c, j - 1], at_z(j))
                for j in range(1, Z)]

    def deg_to_x():
        return [remote(deg_part.at[lax.rem(my_x + j, X)], deg_x.at[j - 1], sem_dx.at[j - 1], at_x(j))
                for j in range(1, X)]

    def deg_to_z():
        return [remote(deg_z.at[my_z], deg_z.at[my_z], sem_dz.at[j - 1], at_z(j)) for j in range(1, Z)]

    def tot_to_z():
        return [remote(tot_z.at[my_z], tot_z.at[my_z], sem_tz.at[j - 1], at_z(j)) for j in range(1, Z)]

    def tot_to_x():
        return [remote(tot_x.at[my_x], tot_x.at[my_x], sem_tx.at[j - 1], at_x(j)) for j in range(1, X)]

    def start(copies):
        for copy in copies:
            copy.start()

    def wait(copies):
        for copy in copies:
            copy.wait()

    barrier = pltpu.get_barrier_semaphore()
    for j in range(1, Z):
        pl.semaphore_signal(barrier, inc=1, device_id={"edge": at_z(j)}, device_id_type=pl.DeviceIdType.MESH)
    for j in range(1, X):
        pl.semaphore_signal(barrier, inc=1, device_id={"edge": at_x(j)}, device_id_type=pl.DeviceIdType.MESH)
    pl.semaphore_wait(barrier, Z + X - 2)

    for c in range(chunks):
        gath[c, my_x, my_z] = dual_ref[c * CH:(c + 1) * CH, :]
        start(agz(c))

    for side in range(2):
        owner = owner_ref[side:side + 1, :]
        row = (owner & (X - 1)) * Z + (owner >> 2)
        own_row[side:side + 1, :] = row
        own_half[side] = jnp.broadcast_to(row.astype(F32), (2 * CH, edges)).astype(BF16)

        def build(j, carry):
            cols = pl.ds(pl.multiple_of(j * 256, 256), 256)
            one = (lax.broadcasted_iota(jnp.int32, (256, 256), 0) == local_ref[side:side + 1, cols]).astype(F32)
            hot[side, :, cols] = one.astype(BF16)
            hot_t[side, cols, :] = one.T.astype(BF16)
            return carry

        lax.fori_loop(0, edges // 256, build, 0)

    for c in range(chunks):
        wait(agz(c))
        start(agx(c))

    degree = None
    for side in range(2):
        rows = lax.broadcasted_iota(jnp.int32, (X * Z, edges), 0)
        named = (rows == own_row[side:side + 1, :]).astype(F32).astype(BF16)
        count = jnp.dot(named, hot_t[side], preferred_element_type=F32)
        degree = count if degree is None else degree + count
    for x in range(X):
        deg_part[x] = degree[x * Z:(x + 1) * Z]
    start(deg_to_x())

    primal_ref[...] = start_ref[...]
    duals_ref[...] = dual_ref[...]
    tot[...] = jnp.zeros_like(tot)
    lane = lax.broadcasted_iota(jnp.int32, (CH, 128), 1)

    def degree_x():
        wait(deg_to_x())
        deg_z[my_z] = deg_part[my_x] + deg_x[0] + deg_x[1] + deg_x[2]
        start(deg_to_z())

    def degree_z():
        wait(deg_to_z())
        total = deg_z[0, pl.ds(my_z, 1), :]
        for z in range(1, Z):
            total = total + deg_z[z, pl.ds(my_z, 1), :]
        step_ref[...] = jnp.broadcast_to(1.0 / jnp.maximum(total, 1.0), step_ref.shape)

    def pull(t):
        c, sweep = lax.rem(t, chunks), lax.div(t, chunks)
        rows = pl.ds(pl.multiple_of(c * CH, CH), CH)
        wait(agx(c))
        high, low = split(gath[c].reshape(X * Z, CH, 256))
        left = jnp.concatenate([high, low], axis=1).reshape(2 * X * Z * CH, 256)
        spend_ref[...] = jnp.zeros_like(spend_ref)

        def block(b, carry):
            cols = pl.ds(pl.multiple_of(b * PULL, PULL), PULL)
            ends = []
            for side in range(2):
                all_rows = jnp.dot(left, hot[side, :, cols], preferred_element_type=F32)
                owner = jnp.broadcast_to(own_row[side:side + 1, cols], (CH, PULL))
                value = jnp.zeros((CH, PULL), F32)
                for o in range(X * Z):
                    at = o * 2 * CH
                    value = jnp.where(owner == o, all_rows[at:at + CH] + all_rows[at + CH:at + 2 * CH], value)
                ends.append(value)
            pulled = ends[0] - ends[1]
            cost, primal = cost_ref[rows, cols], primal_ref[rows, cols]
            moved = jnp.minimum(jnp.maximum(primal - 0.5 * (cost - pulled), 0.0), bound_ref[rows, cols])
            extended = 2.0 * moved - primal
            primal_ref[rows, cols] = moved
            high, low = split(extended)
            both = jnp.concatenate([high, low], axis=0)
            ext[0, :, cols] = both
            ext[1, :, cols] = -both
            spend_ref[...] += jnp.sum(cost * moved, axis=1, keepdims=True)
            return carry

        lax.fori_loop(0, edges // PULL, block, 0)
        tot[rows, :] += jnp.where(lane == ITERS + sweep, jnp.broadcast_to(spend_ref[:, :1], (CH, 128)), 0.0)

    def push(t):
        c = lax.rem(t, chunks)
        total = None
        for side in range(2):
            for b in range(edges // PUSH):
                cols = slice(b * PUSH, (b + 1) * PUSH)
                value = ext[side, :, cols]
                owner = own_half[side, :, cols]
                zero = jnp.zeros_like(value)
                left = jnp.concatenate([jnp.where(owner == BF16(o), value, zero) for o in range(X * Z)], axis=0)
                term = jnp.dot(left, hot_t[side, cols, :], preferred_element_type=F32)
                total = term if total is None else total + term
        for o in range(X * Z):
            at = o * 2 * CH
            part[c, o // Z, o % Z] = total[at:at + CH] + total[at + CH:at + 2 * CH]
        start(to_x(c))

    def stage_a(t):
        c = lax.rem(t, chunks)
        wait(to_x(c))
        zsum[c] = part[c, my_x] + rsx[c, 0] + rsx[c, 1] + rsx[c, 2]
        start(to_z(c))

    def stage_b(t):
        c, sweep = lax.rem(t, chunks), lax.div(t, chunks)
        rows = pl.ds(pl.multiple_of(c * CH, CH), CH)
        wait(to_z(c))
        applied = zsum[c, my_z]
        for j in range(Z - 1):
            applied = applied + rsz[c, j]
        residual = target_ref[rows, :] - applied
        duals = duals_ref[rows, :] + step_ref[...] * residual
        duals_ref[rows, :] = duals
        square = jnp.sum(residual * residual, axis=1, keepdims=True)
        tot[rows, :] += jnp.where(lane == sweep, jnp.broadcast_to(square, (CH, 128)), 0.0)

        @pl.when(sweep < ITERS - 1)
        def _():
            gath[c, my_x, my_z] = duals
            start(agz(c))

    def stage_c(t):
        c, sweep = lax.rem(t, chunks), lax.div(t, chunks)

        @pl.when(sweep < ITERS - 1)
        def _():
            wait(agz(c))
            start(agx(c))

    def slot(t, carry):
        pull(t)

        @pl.when(t == 1)
        def _():
            degree_z()

        @pl.when(t >= 2)
        def _():
            stage_b(t - 2)

        push(t)

        @pl.when(t == 0)
        def _():
            degree_x()

        @pl.when(t >= 1)
        def _():
            stage_a(t - 1)

        @pl.when(t >= 2)
        def _():
            stage_c(t - 2)

        return carry

    lax.fori_loop(0, slots, slot, 0)
    stage_b(slots - 2)
    stage_a(slots - 1)
    stage_b(slots - 1)

    tot_z[my_z] = tot[...]
    start(tot_to_z())
    wait(tot_to_z())
    mine = tot_z[0]
    for z in range(1, Z):
        mine = mine + tot_z[z]
    tot_x[my_x] = mine
    start(tot_to_x())
    wait(tot_to_x())
    totals_ref[...] = (tot_x[0] + tot_x[1]) + (tot_x[2] + tot_x[3])


def body(unit_cost, upper_bound, start_primal, start_dual, net_target, owners, local_ids):
    buckets, edges = unit_cost.shape
    accounts = start_dual.shape[1]
    chunks = buckets // CH
    block = (CH, accounts)
    dma = pltpu.SemaphoreType.DMA
    primal, duals, totals = pl.pallas_call(
        kernel,
        out_shape=(
            jax.ShapeDtypeStruct((buckets, edges), F32),
            jax.ShapeDtypeStruct((buckets, accounts), F32),
            jax.ShapeDtypeStruct((buckets, 128), F32),
        ),
        in_specs=[pl.BlockSpec(memory_space=pltpu.VMEM)] * 7,
        out_specs=[pl.BlockSpec(memory_space=pltpu.VMEM)] * 3,
        scratch_shapes=[
            pltpu.VMEM((2, accounts, edges), BF16),
            pltpu.VMEM((2, edges, accounts), BF16),
            pltpu.VMEM((2, edges), jnp.int32),
            pltpu.VMEM((2, 2 * CH, edges), BF16),
            pltpu.VMEM((2, 2 * CH, edges), BF16),
            pltpu.VMEM((chunks, X, Z) + block, F32),
            pltpu.VMEM((chunks, X, Z) + block, F32),
            pltpu.VMEM((chunks, X - 1, Z) + block, F32),
            pltpu.VMEM((chunks, Z) + block, F32),
            pltpu.VMEM((chunks, Z - 1) + block, F32),
            pltpu.VMEM((X, Z, accounts), F32),
            pltpu.VMEM((X - 1, Z, accounts), F32),
            pltpu.VMEM((Z, Z, accounts), F32),
            pltpu.VMEM(block, F32),
            pltpu.VMEM((CH, 128), F32),
            pltpu.VMEM((buckets, 128), F32),
            pltpu.VMEM((Z, buckets, 128), F32),
            pltpu.VMEM((X, buckets, 128), F32),
            dma((chunks, Z - 1, 2)),
            dma((chunks, X - 1, 2)),
            dma((chunks, X - 1, 2)),
            dma((chunks, Z - 1, 2)),
            dma((X - 1, 2)),
            dma((Z - 1, 2)),
            dma((Z - 1, 2)),
            dma((X - 1, 2)),
        ],
        compiler_params=pltpu.CompilerParams(
            collective_id=0, has_side_effects=True, vmem_limit_bytes=56 * 2**20),
        cost_estimate=pl.CostEstimate(flops=52 * 10**9, bytes_accessed=4 * 2**20, transcendentals=0),
    )(unit_cost, upper_bound, start_primal, start_dual, net_target, owners.T, local_ids.T)
    return primal, duals, totals[:, :2 * ITERS].T.reshape(2, ITERS, buckets)


def solution(mesh):
    return jax.shard_map(
        body,
        mesh=mesh,
        in_specs=(
            P("bucket", "edge"),
            P("bucket", "edge"),
            P("bucket", "edge"),
            P("bucket", "edge"),
            P("bucket", "edge"),
            P("edge", None),
            P("edge", None),
        ),
        out_specs=(P("bucket", "edge"), P("bucket", "edge"), P(None, None, "bucket")),
        check_vma=False,
    )
```

time: 1390 us -> 144 us (0.10)
  waiting for transfers between devices: 1000 us -> 0 us
  other arithmetic: 190 us -> 0 us
  Pallas kernels: 0 us -> 138 us
  local copies, waits for them, and re-layouts: 112 us -> 3.89 us
  blocking collectives: 72.2 us -> 0 us
    reduce_scatter x3 -> x0, waiting for transfers between devices: 659 us -> none  [to_owners(): lax.psum_scatter(partial_value, 'edge', scatter_dimension=1, tiled=True)]
    all_gather x3 -> x0, waiting for transfers between devices: 202 us -> none  [body(): gathered = lax.all_gather(duals, 'edge', axis=1, tiled=True)]
    scatter-add x4 -> x0, other arithmetic: 183 us -> none  [to_owners(): partial_value = jnp.zeros((pushed.shape[0], accounts_here * parties), jnp...]
    unnamed x8 -> x0, waiting for transfers between devices: 140 us -> none
    pallas_call x0 -> x1, Pallas kernels: none -> 138 us  [body(): pl.pallas_call(kernel, out_shape=(jax.ShapeDtypeStruct((buckets, edges),...]
    gather x6 -> x0, local copies, waits for them, and re-layouts: 98.2 us -> none  [body(): values = jnp.take(gathered, global_ids, axis=1)]
    psum x1 -> x0, blocking collectives: 72.2 us -> none  [body(): square_all, spend_all = lax.psum((square_here, spend_here), 'edge')]
  transfers between devices with their start and end apart: 7 -> 0, of which waited for: 7 -> 0; matrix products, arithmetic and copies ran while one was open for 9% -> 0% of each run, Pallas kernels for 0% -> 0%
where the time goes in v1:
time: 144 us; the launch traced here: 143 us
  Pallas kernels  138 us (96%)
  local copies, waits for them, and re-layouts  3.89 us (3%)
    pallas_call x1, Pallas kernels, body(): pl.pallas_call(kernel, out_shape=(jax.ShapeDtypeStruct((buckets, edges),...  138 us
    unnamed x5, local copies, waits for them, and re-layouts  3.08 us

profile of v1, /device:TPU:16, one launch (start us, length us, event | category | flops | bytes accessed | tf_op | source)
XLA Modules:
  0.0 142.8 jit_solution(10876901544183862668)
XLA Ops:
  0.6 138.3 %shard_map.94 = (f32[32,4096]{1,0:T(8,128)}, f32[32,256]{1,0:T(8,128)}, f32[32,128]{1,0:T(8,128)}) custom-call(f32[32,4096]{1,0:T(8,128)} %cost_ref.1, f32[32,4096]{1,0:T(8,128)} %bound_ref.1, f32[32,4096]{1,0:T(8,128)} %start_ref.1, f32[32,256]{1,0:T(8,128)} %dual_ref.1, f32[32,256]{1,0:T(8,128)} %target_ref.1, s32[2,4096]{1,0:T(2,128)} %bitcast.4, ...), custom_call_target="tpu_custom_call" | custom-call | flops 51999997952 | bytes 4194304 | tf_op jit(solution)/shard_map/pallas_call | solution.py:276
  138.9 0.7 slice_bitcast_fusion
  139.6 0.1 copy.11
  139.7 0.6 copy.12
  140.3 0.0 copy-start
  140.3 1.9 %copy.15 = f32[32,4096]{1,0:T(8,128)} copy(f32[32,4096]{1,0:T(8,128)} %get-tuple-element.18) | data formatting | bytes 1048576
  142.2 0.0 copy-done
  142.2 0.6 copy.16
  (1 shorter events, 0.0 us)
Async XLA Ops:
  140.3 1.9 %copy-start = (f32[32,256]{1,0:T(8,128)S(1)}, f32[32,256]{1,0:T(8,128)}, u32[]{:S(2)}) copy-start(f32[32,256]{1,0:T(8,128)} %get-tuple-element.19) | copy-start | bytes 98308

commit v2 on v1

--- a/solution.py
+++ b/solution.py
@@ -12,7 +12,6 @@
 Z = 8
 CH = 8
 PULL = 2048
-PUSH = 4096
 F32 = jnp.float32
 BF16 = jnp.bfloat16
 
@@ -25,8 +24,8 @@
 
 def kernel(cost_ref, bound_ref, start_ref, dual_ref, target_ref, owner_ref, local_ref,
            primal_ref, duals_ref, totals_ref,
-           hot, hot_t, own_row, own_half, ext, gath, part, rsx, zsum, rsz,
-           deg_part, deg_x, deg_z, step_ref, spend_ref, tot, tot_z, tot_x,
+           hot, own_row, own_half, ext, gath, part, rsx, zsum, rsz,
+           deg_part, deg_x, deg_z, step_ref, tot, tot_z, tot_x,
            sem_agz, sem_agx, sem_rsx, sem_rsz, sem_dx, sem_dz, sem_tz, sem_tx):
     edges = cost_ref.shape[1]
     chunks = cost_ref.shape[0] // CH
@@ -104,7 +103,6 @@
             cols = pl.ds(pl.multiple_of(j * 256, 256), 256)
             one = (lax.broadcasted_iota(jnp.int32, (256, 256), 0) == local_ref[side:side + 1, cols]).astype(F32)
             hot[side, :, cols] = one.astype(BF16)
-            hot_t[side, cols, :] = one.T.astype(BF16)
             return carry
 
         lax.fori_loop(0, edges // 256, build, 0)
@@ -117,7 +115,7 @@
     for side in range(2):
         rows = lax.broadcasted_iota(jnp.int32, (X * Z, edges), 0)
         named = (rows == own_row[side:side + 1, :]).astype(F32).astype(BF16)
-        count = jnp.dot(named, hot_t[side], preferred_element_type=F32)
+        count = lax.dot_general(named, hot[side], (((1,), (1,)), ((), ())), preferred_element_type=F32)
         degree = count if degree is None else degree + count
     for x in range(X):
         deg_part[x] = degree[x * Z:(x + 1) * Z]
@@ -140,56 +138,49 @@
             total = total + deg_z[z, pl.ds(my_z, 1), :]
         step_ref[...] = jnp.broadcast_to(1.0 / jnp.maximum(total, 1.0), step_ref.shape)
 
-    def pull(t):
+    def lefts(c):
+        high, low = split(gath[c].reshape(X * Z, CH, 256))
+        return jnp.concatenate([high, low], axis=1).reshape(2 * X * Z * CH, 256)
+
+    def pull(t, b):
         c, sweep = lax.rem(t, chunks), lax.div(t, chunks)
         rows = pl.ds(pl.multiple_of(c * CH, CH), CH)
-        wait(agx(c))
-        high, low = split(gath[c].reshape(X * Z, CH, 256))
-        left = jnp.concatenate([high, low], axis=1).reshape(2 * X * Z * CH, 256)
-        spend_ref[...] = jnp.zeros_like(spend_ref)
-
-        def block(b, carry):
-            cols = pl.ds(pl.multiple_of(b * PULL, PULL), PULL)
-            ends = []
-            for side in range(2):
-                all_rows = jnp.dot(left, hot[side, :, cols], preferred_element_type=F32)
-                owner = jnp.broadcast_to(own_row[side:side + 1, cols], (CH, PULL))
-                value = jnp.zeros((CH, PULL), F32)
-                for o in range(X * Z):
-                    at = o * 2 * CH
-                    value = jnp.where(owner == o, all_rows[at:at + CH] + all_rows[at + CH:at + 2 * CH], value)
-                ends.append(value)
-            pulled = ends[0] - ends[1]
-            cost, primal = cost_ref[rows, cols], primal_ref[rows, cols]
-            moved = jnp.minimum(jnp.maximum(primal - 0.5 * (cost - pulled), 0.0), bound_ref[rows, cols])
-            extended = 2.0 * moved - primal
-            primal_ref[rows, cols] = moved
-            high, low = split(extended)
-            both = jnp.concatenate([high, low], axis=0)
-            ext[0, :, cols] = both
-            ext[1, :, cols] = -both
-            spend_ref[...] += jnp.sum(cost * moved, axis=1, keepdims=True)
-            return carry
-
-        lax.fori_loop(0, edges // PULL, block, 0)
-        tot[rows, :] += jnp.where(lane == ITERS + sweep, jnp.broadcast_to(spend_ref[:, :1], (CH, 128)), 0.0)
-
-    def push(t):
+        cols = slice(b * PULL, (b + 1) * PULL)
+        left = lefts(c)
+        ends = []
+        for side in range(2):
+            all_rows = jnp.dot(left, hot[side, :, cols], preferred_element_type=F32)
+            owner = jnp.broadcast_to(own_row[side:side + 1, cols], (CH, PULL))
+            value = jnp.zeros((CH, PULL), F32)
+            for o in range(X * Z):
+                at = o * 2 * CH
+                value = jnp.where(owner == o, all_rows[at:at + CH] + all_rows[at + CH:at + 2 * CH], value)
+            ends.append(value)
+        pulled = ends[0] - ends[1]
+        cost, primal = cost_ref[rows, cols], primal_ref[rows, cols]
+        moved = jnp.minimum(jnp.maximum(primal - 0.5 * (cost - pulled), 0.0), bound_ref[rows, cols])
+        extended = 2.0 * moved - primal
+        primal_ref[rows, cols] = moved
+        high, low = split(extended)
+        both = jnp.concatenate([high, low], axis=0)
+        ext[0, :, cols] = both
+        ext[1, :, cols] = -both
+        spend = jnp.sum(cost * moved, axis=1, keepdims=True)
+        tot[rows, :] += jnp.where(lane == ITERS + sweep, jnp.broadcast_to(spend, (CH, 128)), 0.0)
+
+    def push(t, side):
         c = lax.rem(t, chunks)
-        total = None
-        for side in range(2):
-            for b in range(edges // PUSH):
-                cols = slice(b * PUSH, (b + 1) * PUSH)
-                value = ext[side, :, cols]
-                owner = own_half[side, :, cols]
-                zero = jnp.zeros_like(value)
-                left = jnp.concatenate([jnp.where(owner == BF16(o), value, zero) for o in range(X * Z)], axis=0)
-                term = jnp.dot(left, hot_t[side, cols, :], preferred_element_type=F32)
-                total = term if total is None else total + term
+        value = ext[side]
+        owner = own_half[side]
+        zero = jnp.zeros_like(value)
+        left = jnp.concatenate([jnp.where(owner == BF16(o), value, zero) for o in range(X * Z)], axis=0)
+        total = lax.dot_general(left, hot[side], (((1,), (1,)), ((), ())), preferred_element_type=F32)
         for o in range(X * Z):
             at = o * 2 * CH
-            part[c, o // Z, o % Z] = total[at:at + CH] + total[at + CH:at + 2 * CH]
-        start(to_x(c))
+            term = total[at:at + CH] + total[at + CH:at + 2 * CH]
+            part[c, o // Z, o % Z] = term if side == 0 else part[c, o // Z, o % Z] + term
+        if side == 1:
+            start(to_x(c))
 
     def stage_a(t):
         c = lax.rem(t, chunks)
@@ -224,7 +215,14 @@
             start(agx(c))
 
     def slot(t, carry):
-        pull(t)
+        wait(agx(lax.rem(t, chunks)))
+        pull(t, 0)
+
+        @pl.when(t >= 3)
+        def _():
+            stage_c(t - 3)
+
+        pull(t, 1)
 
         @pl.when(t == 1)
         def _():
@@ -234,7 +232,7 @@
         def _():
             stage_b(t - 2)
 
-        push(t)
+        push(t, 0)
 
         @pl.when(t == 0)
         def _():
@@ -244,10 +242,7 @@
         def _():
             stage_a(t - 1)
 
-        @pl.when(t >= 2)
-        def _():
-            stage_c(t - 2)
-
+        push(t, 1)
         return carry
 
     lax.fori_loop(0, slots, slot, 0)
@@ -255,7 +250,7 @@
     stage_a(slots - 1)
     stage_b(slots - 1)
 
-    tot_z[my_z] = tot[...]
+    tot_z[my_z] = tot[...].T[:8]
     start(tot_to_z())
     wait(tot_to_z())
     mine = tot_z[0]
@@ -264,7 +259,10 @@
     tot_x[my_x] = mine
     start(tot_to_x())
     wait(tot_to_x())
-    totals_ref[...] = (tot_x[0] + tot_x[1]) + (tot_x[2] + tot_x[3])
+    mine = (tot_x[0] + tot_x[1]) + (tot_x[2] + tot_x[3])
+    for i in range(ITERS):
+        totals_ref[i, 0:1, :] = mine[i:i + 1, :totals_ref.shape[2]]
+        totals_ref[i, 1:2, :] = mine[ITERS + i:ITERS + i + 1, :totals_ref.shape[2]]
 
 
 def body(unit_cost, upper_bound, start_primal, start_dual, net_target, owners, local_ids):
@@ -278,13 +276,12 @@
         out_shape=(
             jax.ShapeDtypeStruct((buckets, edges), F32),
             jax.ShapeDtypeStruct((buckets, accounts), F32),
-            jax.ShapeDtypeStruct((buckets, 128), F32),
+            jax.ShapeDtypeStruct((ITERS, 2, buckets), F32),
         ),
         in_specs=[pl.BlockSpec(memory_space=pltpu.VMEM)] * 7,
         out_specs=[pl.BlockSpec(memory_space=pltpu.VMEM)] * 3,
         scratch_shapes=[
             pltpu.VMEM((2, accounts, edges), BF16),
-            pltpu.VMEM((2, edges, accounts), BF16),
             pltpu.VMEM((2, edges), jnp.int32),
             pltpu.VMEM((2, 2 * CH, edges), BF16),
             pltpu.VMEM((2, 2 * CH, edges), BF16),
@@ -297,10 +294,9 @@
             pltpu.VMEM((X - 1, Z, accounts), F32),
             pltpu.VMEM((Z, Z, accounts), F32),
             pltpu.VMEM(block, F32),
-            pltpu.VMEM((CH, 128), F32),
-            pltpu.VMEM((buckets, 128), F32),
-            pltpu.VMEM((Z, buckets, 128), F32),
-            pltpu.VMEM((X, buckets, 128), F32),
+            pltpu.VMEM((128, 128), F32),
+            pltpu.VMEM((Z, 8, 128), F32),
+            pltpu.VMEM((X, 8, 128), F32),
             dma((chunks, Z - 1, 2)),
             dma((chunks, X - 1, 2)),
             dma((chunks, X - 1, 2)),
@@ -314,7 +310,7 @@
             collective_id=0, has_side_effects=True, vmem_limit_bytes=56 * 2**20),
         cost_estimate=pl.CostEstimate(flops=52 * 10**9, bytes_accessed=4 * 2**20, transcendentals=0),
     )(unit_cost, upper_bound, start_primal, start_dual, net_target, owners.T, local_ids.T)
-    return primal, duals, totals[:, :2 * ITERS].T.reshape(2, ITERS, buckets)
+    return primal, duals, totals.transpose(1, 0, 2)
 
 
 def solution(mesh):

time: 144 us -> 139 us (0.965)
  Pallas kernels: 138 us -> 135 us
    pallas_call x1, Pallas kernels: 138 us -> 135 us  [body(): pl.pallas_call(kernel, out_shape=(jax.ShapeDtypeStruct((buckets, edges),...]
    unnamed x5 -> x7, local copies, waits for them, and re-layouts: 3.08 us -> 3.13 us
where the time goes in v2:
time: 139 us
  Pallas kernels  135 us (97%)
  local copies, waits for them, and re-layouts  3.13 us (2%)
    pallas_call x1, Pallas kernels, body(): pl.pallas_call(kernel, out_shape=(jax.ShapeDtypeStruct((buckets, edges),...  135 us
    unnamed x7, local copies, waits for them, and re-layouts  3.13 us

profile of v2, /device:TPU:16, one launch (start us, length us, event | category | flops | bytes accessed | tf_op | source)
XLA Modules:
  0.0 139.0 jit_solution(15794103026195528468)
XLA Ops:
  0.6 135.2 %shard_map.94 = (f32[32,4096]{1,0:T(8,128)}, f32[32,256]{1,0:T(8,128)}, f32[3,2,32]{2,1,0:T(2,128)}) custom-call(f32[32,4096]{1,0:T(8,128)} %cost_ref.1, f32[32,4096]{1,0:T(8,128)} %bound_ref.1, f32[32,4096]{1,0:T(8,128)} %start_ref.1, f32[32,256]{1,0:T(8,128)} %dual_ref.1, f32[32,256]{1,0:T(8,128)} %target_ref.1, s32[2,4096]{1,0:T(2,128)} %bitcast.4, ...), custom_call_target="tpu_custom_call" | custom-call | flops 51999997952 | bytes 4194304 | tf_op jit(solution)/shard_map/pallas_call | solution.py:274
  135.8 0.0 copy-start
  135.8 1.9 %copy.13 = f32[32,4096]{1,0:T(8,128)} copy(f32[32,4096]{1,0:T(8,128)} %get-tuple-element.12) | data formatting | bytes 1048576
  137.7 0.0 copy-done
  137.7 0.0 copy-start.1
  137.7 0.6 copy.14
  138.3 0.1 copy-done.1
  138.4 0.6 copy.15
Async XLA Ops:
  135.8 1.9 %copy-start = (f32[32,256]{1,0:T(8,128)S(1)}, f32[32,256]{1,0:T(8,128)}, u32[]{:S(2)}) copy-start(f32[32,256]{1,0:T(8,128)} %get-tuple-element.13) | copy-start | bytes 98308
  137.7 0.7 copy-start.1

commit v3 on v0

v3 whole, which is shorter than its diff:
```python
import jax
import jax.numpy as jnp
from jax import lax
from jax.experimental import pallas as pl
from jax.experimental.pallas import tpu as pltpu
from jax.sharding import PartitionSpec as P

ITERS = 3
X = 4
Z = 8
OWNERS = X * Z
HALF = 4
CHUNKS = 2
GROUP = HALF * CHUNKS
LANES = 128
F32 = jnp.float32
BF16 = jnp.bfloat16


def turn(value):
    axis = value.ndim - 2
    first = lax.slice_in_dim(value, 0, HALF, axis=axis)
    second = lax.slice_in_dim(value, HALF, 2 * HALF, axis=axis)
    return jnp.concatenate([second, first], axis=axis)


def kernel(cost_ref, bound_ref, start_ref, dual_ref, target_ref, owner_ref, local_ref,
           primal_ref, duals_ref, totals_ref,
           cost, bound, primal, owner, local, hot, own_half, ext, acc,
           packed, state, gath, part, rsz, deg_part, deg_z, deg_x, step, tot, tot_z, tot_x, back,
           sem_pack, sem_own, sem_loc, sem_cost, sem_bound, sem_primal, sem_agz, sem_rsz,
           sem_dz, sem_dx, sem_tz, sem_tx, sem_back, sem_dual):
    edges = cost_ref.shape[1]
    slots = ITERS * CHUNKS
    me = lax.axis_index("edge")
    my_x = lax.rem(me, X)
    my_z = lax.div(me, X)
    lane = lax.broadcasted_iota(jnp.int32, (GROUP, LANES), 1)
    upper = lax.broadcasted_iota(jnp.int32, (GROUP, LANES), 0) < HALF

    def x_of(j):
        return lax.rem(my_x + j, X)

    def at_x(j):
        return my_z * X + x_of(j)

    def at_z(j):
        return lax.rem(my_z + j, Z) * X + my_x

    def group(x):
        return pl.ds(pl.multiple_of(x * GROUP, GROUP), GROUP)

    def remote(src, dst, send, recv, device):
        return pltpu.make_async_remote_copy(
            src_ref=src, dst_ref=dst, send_sem=send, recv_sem=recv,
            device_id={"edge": device}, device_id_type=pl.DeviceIdType.MESH)

    def give(src, dst, sems, j):
        return remote(src, dst.at[X - j], sems.at[0, j], sems.at[1, X - j], at_x(j))

    def give_rows(src, dst, sems, j):
        return give(src.at[group(x_of(j))], dst, sems, j)

    def taken(dst, sems, j):
        return remote(dst.at[j], dst.at[j], sems.at[0, j], sems.at[1, j], at_x(j))

    def packs(j):
        return give(packed.at[x_of(j)], state, sem_pack, j)

    def agz(c):
        block = gath.at[c, my_z]
        return [remote(block, block, sem_agz.at[c, 0, j], sem_agz.at[c, 1, j], at_z(j)) for j in range(1, Z)]

    def to_z(c):
        return [remote(part.at[c, lax.rem(my_z + j, Z)], rsz.at[c, j - 1], sem_rsz.at[c, 0, j], sem_rsz.at[c, 1, j],
                       at_z(j)) for j in range(1, Z)]

    def deg_to_z():
        return [remote(deg_part.at[lax.rem(my_z + j, Z)], deg_z.at[j - 1], sem_dz.at[0, j], sem_dz.at[1, j], at_z(j))
                for j in range(1, Z)]

    def deg_to_x():
        return [give(deg_x.at[0], deg_x, sem_dx, j) for j in range(1, X)]

    def tot_to_z():
        return [remote(tot_z.at[my_z], tot_z.at[my_z], sem_tz.at[0, j], sem_tz.at[1, j], at_z(j))
                for j in range(1, Z)]

    def tot_to_x():
        return [remote(tot_x.at[my_x], tot_x.at[my_x], sem_tx.at[0, j], sem_tx.at[1, X - j], at_x(j))
                for j in range(1, X)]

    def primal_back(j):
        return remote(primal.at[j], primal_ref.at[group(my_x)], sem_back.at[0, j], sem_back.at[1, X - j], at_x(j))

    def dual_back(j):
        return remote(back.at[j], duals_ref.at[group(my_x)], sem_dual.at[0, j], sem_dual.at[1, X - j], at_x(j))

    def start(copies):
        for copy in copies:
            copy.start()

    def wait(copies):
        for copy in copies:
            copy.wait()

    for g in range(X):
        for kind, ref in enumerate((dual_ref, target_ref)):
            rows = ref[g * GROUP:(g + 1) * GROUP, :]
            low, high = rows[:, :LANES], rows[:, LANES:]
            packed[g, 2 * kind] = jnp.concatenate([low[:HALF], high[:HALF]], axis=0)
            packed[g, 2 * kind + 1] = jnp.concatenate([low[HALF:], high[HALF:]], axis=0)

    barrier = pltpu.get_barrier_semaphore()
    for j in range(1, Z):
        pl.semaphore_signal(barrier, inc=1, device_id={"edge": at_z(j)}, device_id_type=pl.DeviceIdType.MESH)
    for j in range(1, X):
        pl.semaphore_signal(barrier, inc=1, device_id={"edge": at_x(j)}, device_id_type=pl.DeviceIdType.MESH)
    pl.semaphore_wait(barrier, Z + X - 2)

    peers = (3, 1, 2)
    for j in peers:
        packs(j).start()
    for j in peers:
        give(owner_ref, owner, sem_own, j).start()
        give(local_ref, local, sem_loc, j).start()
    for j in peers:
        give_rows(cost_ref, cost, sem_cost, j).start()
        give_rows(bound_ref, bound, sem_bound, j).start()
        give_rows(start_ref, primal, sem_primal, j).start()

    state[0] = packed[my_x]
    owner[0] = owner_ref[...]
    local[0] = local_ref[...]
    cost[0] = cost_ref[group(my_x), :]
    bound[0] = bound_ref[group(my_x), :]
    primal[0] = start_ref[group(my_x), :]

    def build(j):
        second = lax.broadcasted_iota(jnp.int32, (2 * GROUP, 256), 0) >= GROUP

        def some(b, carry):
            here = pl.ds(pl.multiple_of(b * 256, 256), 256)
            cols = pl.ds(pl.multiple_of(j * edges + b * 256, 256), 256)
            for side in range(2):
                ids = local[j, side:side + 1, here]
                one = (lax.broadcasted_iota(jnp.int32, (256, 256), 0) == ids).astype(F32)
                hot[side, :, cols] = one.astype(BF16)
                names = jnp.broadcast_to(owner[j, side:side + 1, here], (2 * GROUP, 256))
                own_half[side, :, cols] = jnp.where(second, names - 1, names).astype(F32).astype(BF16)
            return carry

        lax.fori_loop(0, edges // 256, some, 0)

    build(0)
    for j in peers:
        packs(j).wait()
    for c in range(CHUNKS):
        for x in range(X):
            gath[c, my_z, x] = state[lax.rem(x + X - my_x, X), c]
        start(agz(c))

    degree = None
    for side in range(2):
        rows = lax.broadcasted_iota(jnp.int32, (OWNERS, edges), 0)
        named = (rows == owner_ref[side:side + 1, :]).astype(F32).astype(BF16)
        count = lax.dot_general(named, hot[side, :, :edges], (((1,), (1,)), ((), ())), preferred_element_type=F32)
        degree = count if degree is None else degree + count
    for z in range(Z):
        four = degree[z * X:(z + 1) * X]
        deg_part[z] = jnp.concatenate([four, four], axis=0)
    start(deg_to_z())
    tot[...] = jnp.zeros_like(tot)

    for j in peers:
        give(owner_ref, owner, sem_own, j).wait()
        give(local_ref, local, sem_loc, j).wait()

    def later(j, carry):
        build(j)
        return carry

    lax.fori_loop(1, X, later, 0)

    wait(deg_to_z())
    mine = deg_part[my_z]
    for j in range(Z - 1):
        mine = mine + deg_z[j]
    deg_x[0] = mine
    start(deg_to_x())

    def degree_done():
        wait(deg_to_x())
        whole = (deg_x[0] + deg_x[1]) + (deg_x[2] + deg_x[3])
        inverse = 1.0 / jnp.maximum(whole, 1.0)
        for x in range(X):
            low = jnp.broadcast_to(inverse[x:x + 1, :LANES], (GROUP, LANES))
            high = jnp.broadcast_to(inverse[x:x + 1, LANES:], (GROUP, LANES))
            step[x] = jnp.where(upper, low, high)

    def pull(t):
        c, sweep = lax.rem(t, CHUNKS), lax.div(t, CHUNKS)
        wait(agz(c))
        value = gath[c].reshape(OWNERS, GROUP, LANES)
        high = value.astype(BF16).astype(F32)
        low = value - high
        is_upper = lax.broadcasted_iota(jnp.int32, (OWNERS, GROUP, LANES), 1) < HALF
        first = jnp.where(is_upper, high, turn(low))
        second = jnp.where(is_upper, turn(high), low)
        left = jnp.concatenate([first, second], axis=2).reshape(OWNERS * GROUP, 2 * LANES).astype(BF16)
        in_upper = lax.broadcasted_iota(jnp.int32, (GROUP, edges), 0) < HALF
        in_chunk = (lax.broadcasted_iota(jnp.int32, (GROUP, edges), 0) >= HALF) == (c == 1)

        def block(j, spend):
            @pl.when((t == 0) & (j > 0))
            def _():
                taken(cost, sem_cost, j).wait_recv()
                taken(bound, sem_bound, j).wait_recv()
                taken(primal, sem_primal, j).wait_recv()

            cols = pl.ds(pl.multiple_of(j * edges, edges), edges)
            ends = []
            for side in range(2):
                all_rows = jnp.dot(left, hot[side, :, cols], preferred_element_type=F32)
                names = jnp.broadcast_to(owner[j, side:side + 1, :], (GROUP, edges))
                found = jnp.zeros((GROUP, edges), F32)
                for o in range(OWNERS):
                    found = jnp.where(names == o, all_rows[o * GROUP:(o + 1) * GROUP], found)
                ends.append(found)
            pulled = ends[0] - ends[1]
            pulled = pulled + turn(pulled)
            price, before = cost[j], primal[j]
            moved = jnp.minimum(jnp.maximum(before - 0.5 * (price - pulled), 0.0), bound[j])
            primal[j] = jnp.where(in_chunk, moved, before)
            extended = jnp.where(in_chunk, 2.0 * moved - before, 0.0)
            extended = extended + turn(extended)
            high = extended.astype(BF16).astype(F32)
            both = jnp.where(in_upper, high, extended - high)
            both = jnp.concatenate([both, both], axis=0).astype(BF16)
            ext[0, :, cols] = both
            ext[1, :, cols] = -both

            @pl.when((t == slots - 1) & (j > 0))
            def _():
                primal_back(j).start()

            return spend + jnp.sum(jnp.where(in_chunk, price * moved, 0.0), axis=1, keepdims=True)

        spend = lax.fori_loop(0, X, block, jnp.zeros((GROUP, 1), F32))
        tot[...] += jnp.where(lane == ITERS + sweep, jnp.broadcast_to(spend, (GROUP, LANES)), 0.0)

    def push(t):
        c = lax.rem(t, CHUNKS)
        acc[...] = jnp.zeros_like(acc)

        def block(j, carry):
            cols = pl.ds(pl.multiple_of(j * edges, edges), edges)
            for side in range(2):
                value, names = ext[side, :, cols], own_half[side, :, cols]
                zero = jnp.zeros_like(value)
                left = jnp.concatenate(
                    [jnp.where(names == BF16(o), value, zero) for o in range(0, OWNERS, 2)], axis=0)
                acc[...] += lax.dot_general(left, hot[side, :, cols], (((1,), (1,)), ((), ())),
                                            preferred_element_type=F32)
            return carry

        lax.fori_loop(0, X, block, 0)
        value = acc[...].reshape(OWNERS, GROUP, 2 * LANES)
        value = value + turn(value)
        is_upper = lax.broadcasted_iota(jnp.int32, (OWNERS, GROUP, LANES), 1) < HALF
        part[c] = jnp.where(is_upper, value[:, :, :LANES], value[:, :, LANES:]).reshape(Z, X, GROUP, LANES)
        start(to_z(c))

    def settle(t):
        c, sweep = lax.rem(t, CHUNKS), lax.div(t, CHUNKS)
        wait(to_z(c))
        squares = jnp.zeros((GROUP, LANES), F32)
        for x in range(X):
            place = lax.rem(x + X - my_x, X)
            applied = part[c, my_z, x]
            for j in range(Z - 1):
                applied = applied + rsz[c, j, x]
            residual = state[place, CHUNKS + c] - applied
            duals = state[place, c] + step[x] * residual
            state[place, c] = duals
            gath[c, my_z, x] = duals
            squares = squares + residual * residual
        square = jnp.broadcast_to(jnp.sum(squares, axis=1, keepdims=True), (GROUP, LANES))
        square = square + turn(square)
        tot[...] += jnp.where((lane == sweep) & (upper == (c == 0)), square, 0.0)

        @pl.when(sweep < ITERS - 1)
        def _():
            start(agz(c))

    def slot(t, carry):
        pull(t)

        @pl.when(t == 1)
        def _():
            degree_done()

        @pl.when(t >= 1)
        def _():
            settle(t - 1)

        push(t)
        return carry

    lax.fori_loop(0, slots, slot, 0)
    settle(slots - 1)

    tot_z[my_z] = tot[...]
    start(tot_to_z())
    for j in range(X):
        first, second = state[j, 0], state[j, 1]
        back[j] = jnp.concatenate(
            [jnp.concatenate([first[:HALF], second[:HALF]], axis=0),
             jnp.concatenate([first[HALF:], second[HALF:]], axis=0)], axis=1)
    for j in peers:
        dual_back(j).start()
    duals_ref[group(my_x), :] = back[0]
    primal_ref[group(my_x), :] = primal[0]
    for j in peers:
        give_rows(cost_ref, cost, sem_cost, j).wait_send()
        give_rows(bound_ref, bound, sem_bound, j).wait_send()
        give_rows(start_ref, primal, sem_primal, j).wait_send()
    wait(tot_to_z())
    mine = tot_z[0]
    for z in range(1, Z):
        mine = mine + tot_z[z]
    tot_x[my_x] = mine
    start(tot_to_x())
    wait([primal_back(j) for j in peers])
    wait([dual_back(j) for j in peers])
    wait(tot_to_x())
    every = jnp.concatenate([tot_x[x] for x in range(X)] + [jnp.zeros((LANES - X * GROUP, LANES), F32)], axis=0).T
    for i in range(ITERS):
        totals_ref[i, 0:1, :] = every[i:i + 1, :X * GROUP]
        totals_ref[i, 1:2, :] = every[ITERS + i:ITERS + i + 1, :X * GROUP]


def body(unit_cost, upper_bound, start_primal, start_dual, net_target, owners, local_ids):
    buckets, edges = unit_cost.shape
    accounts = start_dual.shape[1]
    tile = (GROUP, LANES)
    dma = pltpu.SemaphoreType.DMA
    vmem = pltpu.VMEM
    primal, duals, totals = pl.pallas_call(
        kernel,
        out_shape=(
            jax.ShapeDtypeStruct((buckets, edges), F32),
            jax.ShapeDtypeStruct((buckets, accounts), F32),
            jax.ShapeDtypeStruct((ITERS, 2, buckets), F32),
        ),
        in_specs=[pl.BlockSpec(memory_space=vmem)] * 7,
        out_specs=[pl.BlockSpec(memory_space=vmem)] * 3,
        scratch_shapes=[
            vmem((X, GROUP, edges), F32),
            vmem((X, GROUP, edges), F32),
            vmem((X, GROUP, edges), F32),
            vmem((X, 2, edges), jnp.int32),
            vmem((X, 2, edges), jnp.int32),
            vmem((2, accounts, X * edges), BF16),
            vmem((2, 2 * GROUP, X * edges), BF16),
            vmem((2, 2 * GROUP, X * edges), BF16),
            vmem((OWNERS * GROUP, accounts), F32),
            vmem((X, 2 * CHUNKS) + tile, F32),
            vmem((X, 2 * CHUNKS) + tile, F32),
            vmem((CHUNKS, Z, X) + tile, F32),
            vmem((CHUNKS, Z, X) + tile, F32),
            vmem((CHUNKS, Z - 1, X) + tile, F32),
            vmem((Z, GROUP, accounts), F32),
            vmem((Z - 1, GROUP, accounts), F32),
            vmem((X, GROUP, accounts), F32),
            vmem((X,) + tile, F32),
            vmem(tile, F32),
            vmem((Z,) + tile, F32),
            vmem((X,) + tile, F32),
            vmem((X, GROUP, accounts), F32),
            dma((2, X)),
            dma((2, X)),
            dma((2, X)),
            dma((2, X)),
            dma((2, X)),
            dma((2, X)),
            dma((CHUNKS, 2, Z)),
            dma((CHUNKS, 2, Z)),
            dma((2, Z)),
            dma((2, X)),
            dma((2, Z)),
            dma((2, X)),
            dma((2, X)),
            dma((2, X)),
        ],
        compiler_params=pltpu.CompilerParams(
            collective_id=0, has_side_effects=True, vmem_limit_bytes=58 * 2**20),
        cost_estimate=pl.CostEstimate(flops=52 * 10**9, bytes_accessed=4 * 2**20, transcendentals=0),
    )(unit_cost, upper_bound, start_primal, start_dual, net_target, owners.T, local_ids.T)
    return primal, duals, totals.transpose(1, 0, 2)


def solution(mesh):
    return jax.shard_map(
        body,
        mesh=mesh,
        in_specs=(
            P("bucket", "edge"),
            P("bucket", "edge"),
            P("bucket", "edge"),
            P("bucket", "edge"),
            P("bucket", "edge"),
            P("edge", None),
            P("edge", None),
        ),
        out_specs=(P("bucket", "edge"), P("bucket", "edge"), P(None, None, "bucket")),
        check_vma=False,
    )
```

time: 1390 us -> 116 us (0.08)
  waiting for transfers between devices: 1000 us -> 0 us
  other arithmetic: 190 us -> 0 us
  Pallas kernels: 0 us -> 112 us
  local copies, waits for them, and re-layouts: 112 us -> 3.13 us
  blocking collectives: 72.2 us -> 0 us
    reduce_scatter x3 -> x0, waiting for transfers between devices: 659 us -> none  [to_owners(): lax.psum_scatter(partial_value, 'edge', scatter_dimension=1, tiled=True)]
    all_gather x3 -> x0, waiting for transfers between devices: 202 us -> none  [body(): gathered = lax.all_gather(duals, 'edge', axis=1, tiled=True)]
    scatter-add x4 -> x0, other arithmetic: 183 us -> none  [to_owners(): partial_value = jnp.zeros((pushed.shape[0], accounts_here * parties), jnp...]
    unnamed x8 -> x0, waiting for transfers between devices: 140 us -> none
    pallas_call x0 -> x1, Pallas kernels: none -> 112 us  [body(): pl.pallas_call(kernel, out_shape=(jax.ShapeDtypeStruct((buckets, edges),...]
    gather x6 -> x0, local copies, waits for them, and re-layouts: 98.2 us -> none  [body(): values = jnp.take(gathered, global_ids, axis=1)]
    psum x1 -> x0, blocking collectives: 72.2 us -> none  [body(): square_all, spend_all = lax.psum((square_here, spend_here), 'edge')]
  transfers between devices with their start and end apart: 7 -> 0, of which waited for: 7 -> 0; matrix products, arithmetic and copies ran while one was open for 9% -> 0% of each run, Pallas kernels for 0% -> 0%
where the time goes in v3:
time: 116 us
  Pallas kernels  112 us (97%)
  local copies, waits for them, and re-layouts  3.13 us (3%)
    pallas_call x1, Pallas kernels, body(): pl.pallas_call(kernel, out_shape=(jax.ShapeDtypeStruct((buckets, edges),...  112 us
    unnamed x7, local copies, waits for them, and re-layouts  3.13 us

profile of v3, /device:TPU:16, one launch (start us, length us, event | category | flops | bytes accessed | tf_op | source)
XLA Modules:
  0.0 115.7 jit_solution(2829891340600982520)
XLA Ops:
  0.6 111.9 %shard_map.94 = (f32[32,4096]{1,0:T(8,128)}, f32[32,256]{1,0:T(8,128)}, f32[3,2,32]{2,1,0:T(2,128)}) custom-call(f32[32,4096]{1,0:T(8,128)} %cost_ref.1, f32[32,4096]{1,0:T(8,128)} %bound_ref.1, f32[32,4096]{1,0:T(8,128)} %start_ref.1, f32[32,256]{1,0:T(8,128)} %dual_ref.1, f32[32,256]{1,0:T(8,128)} %target_ref.1, s32[2,4096]{1,0:T(2,128)} %bitcast.4, ...), custom_call_target="tpu_custom_call" | custom-call | flops 51999997952 | bytes 4194304 | tf_op jit(solution)/shard_map/pallas_call | solution.py:349
  112.5 0.0 copy-start
  112.5 1.9 %copy.13 = f32[32,4096]{1,0:T(8,128)} copy(f32[32,4096]{1,0:T(8,128)} %get-tuple-element.12) | data formatting | bytes 1048576
  114.4 0.0 copy-done
  114.4 0.0 copy-start.1
  114.4 0.6 copy.14
  115.0 0.1 copy-done.1
  115.1 0.6 copy.15
Async XLA Ops:
  112.5 1.9 %copy-start = (f32[32,256]{1,0:T(8,128)S(1)}, f32[32,256]{1,0:T(8,128)}, u32[]{:S(2)}) copy-start(f32[32,256]{1,0:T(8,128)} %get-tuple-element.13) | copy-start | bytes 98308
  114.4 0.7 copy-start.1

commit v4 on v3

--- a/solution.py
+++ b/solution.py
@@ -9,6 +9,7 @@
 X = 4
 Z = 8
 OWNERS = X * Z
+FAR = (4, 3, 5, 2, 6, 1, 7)
 HALF = 4
 CHUNKS = 2
 GROUP = HALF * CHUNKS
@@ -26,7 +27,7 @@
 
 def kernel(cost_ref, bound_ref, start_ref, dual_ref, target_ref, owner_ref, local_ref,
            primal_ref, duals_ref, totals_ref,
-           cost, bound, primal, owner, local, hot, own_half, ext, acc,
+           cost, bound, primal, owner, local, hot, own_half, ext, left, acc,
            packed, state, gath, part, rsz, deg_part, deg_z, deg_x, step, tot, tot_z, tot_x, back,
            sem_pack, sem_own, sem_loc, sem_cost, sem_bound, sem_primal, sem_agz, sem_rsz,
            sem_dz, sem_dx, sem_tz, sem_tx, sem_back, sem_dual):
@@ -69,11 +70,11 @@
 
     def agz(c):
         block = gath.at[c, my_z]
-        return [remote(block, block, sem_agz.at[c, 0, j], sem_agz.at[c, 1, j], at_z(j)) for j in range(1, Z)]
+        return [remote(block, block, sem_agz.at[c, 0, j], sem_agz.at[c, 1, j], at_z(j)) for j in FAR]
 
     def to_z(c):
         return [remote(part.at[c, lax.rem(my_z + j, Z)], rsz.at[c, j - 1], sem_rsz.at[c, 0, j], sem_rsz.at[c, 1, j],
-                       at_z(j)) for j in range(1, Z)]
+                       at_z(j)) for j in FAR]
 
     def deg_to_z():
         return [remote(deg_part.at[lax.rem(my_z + j, Z)], deg_z.at[j - 1], sem_dz.at[0, j], sem_dz.at[1, j], at_z(j))
@@ -119,15 +120,16 @@
     pl.semaphore_wait(barrier, Z + X - 2)
 
     peers = (3, 1, 2)
+
+    def give_arrays(j):
+        return [give_rows(cost_ref, cost, sem_cost, j), give_rows(bound_ref, bound, sem_bound, j),
+                give_rows(start_ref, primal, sem_primal, j)]
+
     for j in peers:
         packs(j).start()
     for j in peers:
         give(owner_ref, owner, sem_own, j).start()
         give(local_ref, local, sem_loc, j).start()
-    for j in peers:
-        give_rows(cost_ref, cost, sem_cost, j).start()
-        give_rows(bound_ref, bound, sem_bound, j).start()
-        give_rows(start_ref, primal, sem_primal, j).start()
 
     state[0] = packed[my_x]
     owner[0] = owner_ref[...]
@@ -152,13 +154,14 @@
 
         lax.fori_loop(0, edges // 256, some, 0)
 
-    build(0)
     for j in peers:
         packs(j).wait()
     for c in range(CHUNKS):
         for x in range(X):
             gath[c, my_z, x] = state[lax.rem(x + X - my_x, X), c]
         start(agz(c))
+    start(give_arrays(3) + give_arrays(1))
+    build(0)
 
     degree = None
     for side in range(2):
@@ -175,6 +178,7 @@
     for j in peers:
         give(owner_ref, owner, sem_own, j).wait()
         give(local_ref, local, sem_loc, j).wait()
+    start(give_arrays(2))
 
     def later(j, carry):
         build(j)
@@ -197,79 +201,6 @@
             low = jnp.broadcast_to(inverse[x:x + 1, :LANES], (GROUP, LANES))
             high = jnp.broadcast_to(inverse[x:x + 1, LANES:], (GROUP, LANES))
             step[x] = jnp.where(upper, low, high)
-
-    def pull(t):
-        c, sweep = lax.rem(t, CHUNKS), lax.div(t, CHUNKS)
-        wait(agz(c))
-        value = gath[c].reshape(OWNERS, GROUP, LANES)
-        high = value.astype(BF16).astype(F32)
-        low = value - high
-        is_upper = lax.broadcasted_iota(jnp.int32, (OWNERS, GROUP, LANES), 1) < HALF
-        first = jnp.where(is_upper, high, turn(low))
-        second = jnp.where(is_upper, turn(high), low)
-        left = jnp.concatenate([first, second], axis=2).reshape(OWNERS * GROUP, 2 * LANES).astype(BF16)
-        in_upper = lax.broadcasted_iota(jnp.int32, (GROUP, edges), 0) < HALF
-        in_chunk = (lax.broadcasted_iota(jnp.int32, (GROUP, edges), 0) >= HALF) == (c == 1)
-
-        def block(j, spend):
-            @pl.when((t == 0) & (j > 0))
-            def _():
-                taken(cost, sem_cost, j).wait_recv()
-                taken(bound, sem_bound, j).wait_recv()
-                taken(primal, sem_primal, j).wait_recv()
-
-            cols = pl.ds(pl.multiple_of(j * edges, edges), edges)
-            ends = []
-            for side in range(2):
-                all_rows = jnp.dot(left, hot[side, :, cols], preferred_element_type=F32)
-                names = jnp.broadcast_to(owner[j, side:side + 1, :], (GROUP, edges))
-                found = jnp.zeros((GROUP, edges), F32)
-                for o in range(OWNERS):
-                    found = jnp.where(names == o, all_rows[o * GROUP:(o + 1) * GROUP], found)
-                ends.append(found)
-            pulled = ends[0] - ends[1]
-            pulled = pulled + turn(pulled)
-            price, before = cost[j], primal[j]
-            moved = jnp.minimum(jnp.maximum(before - 0.5 * (price - pulled), 0.0), bound[j])
-            primal[j] = jnp.where(in_chunk, moved, before)
-            extended = jnp.where(in_chunk, 2.0 * moved - before, 0.0)
-            extended = extended + turn(extended)
-            high = extended.astype(BF16).astype(F32)
-            both = jnp.where(in_upper, high, extended - high)
-            both = jnp.concatenate([both, both], axis=0).astype(BF16)
-            ext[0, :, cols] = both
-            ext[1, :, cols] = -both
-
-            @pl.when((t == slots - 1) & (j > 0))
-            def _():
-                primal_back(j).start()
-
-            return spend + jnp.sum(jnp.where(in_chunk, price * moved, 0.0), axis=1, keepdims=True)
-
-        spend = lax.fori_loop(0, X, block, jnp.zeros((GROUP, 1), F32))
-        tot[...] += jnp.where(lane == ITERS + sweep, jnp.broadcast_to(spend, (GROUP, LANES)), 0.0)
-
-    def push(t):
-        c = lax.rem(t, CHUNKS)
-        acc[...] = jnp.zeros_like(acc)
-
-        def block(j, carry):
-            cols = pl.ds(pl.multiple_of(j * edges, edges), edges)
-            for side in range(2):
-                value, names = ext[side, :, cols], own_half[side, :, cols]
-                zero = jnp.zeros_like(value)
-                left = jnp.concatenate(
-                    [jnp.where(names == BF16(o), value, zero) for o in range(0, OWNERS, 2)], axis=0)
-                acc[...] += lax.dot_general(left, hot[side, :, cols], (((1,), (1,)), ((), ())),
-                                            preferred_element_type=F32)
-            return carry
-
-        lax.fori_loop(0, X, block, 0)
-        value = acc[...].reshape(OWNERS, GROUP, 2 * LANES)
-        value = value + turn(value)
-        is_upper = lax.broadcasted_iota(jnp.int32, (OWNERS, GROUP, LANES), 1) < HALF
-        part[c] = jnp.where(is_upper, value[:, :, :LANES], value[:, :, LANES:]).reshape(Z, X, GROUP, LANES)
-        start(to_z(c))
 
     def settle(t):
         c, sweep = lax.rem(t, CHUNKS), lax.div(t, CHUNKS)
@@ -294,17 +225,77 @@
             start(agz(c))
 
     def slot(t, carry):
-        pull(t)
-
-        @pl.when(t == 1)
-        def _():
-            degree_done()
-
-        @pl.when(t >= 1)
-        def _():
-            settle(t - 1)
-
-        push(t)
+        c, sweep = lax.rem(t, CHUNKS), lax.div(t, CHUNKS)
+        wait(agz(c))
+        value = gath[c].reshape(OWNERS, GROUP, LANES)
+        high = value.astype(BF16).astype(F32)
+        low = value - high
+        is_upper = lax.broadcasted_iota(jnp.int32, (OWNERS, GROUP, LANES), 1) < HALF
+        first = jnp.where(is_upper, high, turn(low))
+        second = jnp.where(is_upper, turn(high), low)
+        left[...] = jnp.concatenate([first, second], axis=2).reshape(OWNERS * GROUP, 2 * LANES).astype(BF16)
+        in_upper = lax.broadcasted_iota(jnp.int32, (GROUP, edges), 0) < HALF
+        in_chunk = (lax.broadcasted_iota(jnp.int32, (GROUP, edges), 0) >= HALF) == (c == 1)
+        acc[...] = jnp.zeros_like(acc)
+
+        def block(i, spend):
+            j = jnp.where(i < 2, i, 5 - i)
+
+            @pl.when((t == 0) & (i > 0))
+            def _():
+                taken(cost, sem_cost, j).wait_recv()
+                taken(bound, sem_bound, j).wait_recv()
+                taken(primal, sem_primal, j).wait_recv()
+
+            @pl.when((t == 1) & (i == 2))
+            def _():
+                degree_done()
+
+            @pl.when((t >= 1) & (i == 2))
+            def _():
+                settle(t - 1)
+
+            cols = pl.ds(pl.multiple_of(j * edges, edges), edges)
+            ends = []
+            for side in range(2):
+                all_rows = jnp.dot(left[...], hot[side, :, cols], preferred_element_type=F32)
+                names = jnp.broadcast_to(owner[j, side:side + 1, :], (GROUP, edges))
+                found = jnp.zeros((GROUP, edges), F32)
+                for o in range(OWNERS):
+                    found = jnp.where(names == o, all_rows[o * GROUP:(o + 1) * GROUP], found)
+                ends.append(found)
+            pulled = ends[0] - ends[1]
+            pulled = pulled + turn(pulled)
+            price, before = cost[j], primal[j]
+            moved = jnp.minimum(jnp.maximum(before - 0.5 * (price - pulled), 0.0), bound[j])
+            primal[j] = jnp.where(in_chunk, moved, before)
+            extended = jnp.where(in_chunk, 2.0 * moved - before, 0.0)
+            extended = extended + turn(extended)
+            high = extended.astype(BF16).astype(F32)
+            both = jnp.where(in_upper, high, extended - high)
+            both = jnp.concatenate([both, both], axis=0).astype(BF16)
+            ext[0] = both
+            ext[1] = -both
+
+            @pl.when((t == slots - 1) & (i > 0))
+            def _():
+                primal_back(j).start()
+
+            for side in range(2):
+                value, names = ext[side], own_half[side, :, cols]
+                zero = jnp.zeros_like(value)
+                masked = jnp.concatenate(
+                    [jnp.where(names == BF16(o), value, zero) for o in range(0, OWNERS, 2)], axis=0)
+                acc[...] += lax.dot_general(masked, hot[side, :, cols], (((1,), (1,)), ((), ())),
+                                            preferred_element_type=F32)
+            return spend + jnp.sum(jnp.where(in_chunk, price * moved, 0.0), axis=1, keepdims=True)
+
+        spend = lax.fori_loop(0, X, block, jnp.zeros((GROUP, 1), F32))
+        tot[...] += jnp.where(lane == ITERS + sweep, jnp.broadcast_to(spend, (GROUP, LANES)), 0.0)
+        value = acc[...].reshape(OWNERS, GROUP, 2 * LANES)
+        value = value + turn(value)
+        part[c] = jnp.where(is_upper, value[:, :, :LANES], value[:, :, LANES:]).reshape(Z, X, GROUP, LANES)
+        start(to_z(c))
         return carry
 
     lax.fori_loop(0, slots, slot, 0)
@@ -322,9 +313,8 @@
     duals_ref[group(my_x), :] = back[0]
     primal_ref[group(my_x), :] = primal[0]
     for j in peers:
-        give_rows(cost_ref, cost, sem_cost, j).wait_send()
-        give_rows(bound_ref, bound, sem_bound, j).wait_send()
-        give_rows(start_ref, primal, sem_primal, j).wait_send()
+        for copy in give_arrays(j):
+            copy.wait_send()
     wait(tot_to_z())
     mine = tot_z[0]
     for z in range(1, Z):
@@ -338,6 +328,16 @@
     for i in range(ITERS):
         totals_ref[i, 0:1, :] = every[i:i + 1, :X * GROUP]
         totals_ref[i, 1:2, :] = every[ITERS + i:ITERS + i + 1, :X * GROUP]
+
+
+def finish(*refs):
+    count = len(refs) // 2
+    sems = refs[-1]
+    copies = [pltpu.make_async_copy(refs[i], refs[count + i], sems.at[i]) for i in range(count)]
+    for copy in copies:
+        copy.start()
+    for copy in copies:
+        copy.wait()
 
 
 def body(unit_cost, upper_bound, start_primal, start_dual, net_target, owners, local_ids):
@@ -363,7 +363,8 @@
             vmem((X, 2, edges), jnp.int32),
             vmem((2, accounts, X * edges), BF16),
             vmem((2, 2 * GROUP, X * edges), BF16),
-            vmem((2, 2 * GROUP, X * edges), BF16),
+            vmem((2, 2 * GROUP, edges), BF16),
+            vmem((OWNERS * GROUP, accounts), BF16),
             vmem((OWNERS * GROUP, accounts), F32),
             vmem((X, 2 * CHUNKS) + tile, F32),
             vmem((X, 2 * CHUNKS) + tile, F32),
@@ -397,6 +398,15 @@
             collective_id=0, has_side_effects=True, vmem_limit_bytes=58 * 2**20),
         cost_estimate=pl.CostEstimate(flops=52 * 10**9, bytes_accessed=4 * 2**20, transcendentals=0),
     )(unit_cost, upper_bound, start_primal, start_dual, net_target, owners.T, local_ids.T)
+    results = (primal, duals, totals)
+    primal, duals, totals = pl.pallas_call(
+        finish,
+        out_shape=tuple(jax.ShapeDtypeStruct(r.shape, r.dtype) for r in results),
+        in_specs=[pl.BlockSpec(memory_space=pl.ANY)] * 3,
+        out_specs=[pl.BlockSpec(memory_space=pl.ANY)] * 3,
+        scratch_shapes=[dma((3,))],
+        compiler_params=pltpu.CompilerParams(vmem_limit_bytes=60 * 2**20),
+    )(*results)
     return primal, duals, totals.transpose(1, 0, 2)
 
 

time: 116 us -> 168 us (1.45)
  Pallas kernels: 112 us -> 167 us
  local copies, waits for them, and re-layouts: 3.13 us -> 0 us
    pallas_call x1, Pallas kernels: 112 us -> 149 us  [body(): pl.pallas_call(kernel, out_shape=(jax.ShapeDtypeStruct((buckets, edges),...]
    pallas_call x0 -> x1, Pallas kernels: none -> 18.1 us  [body(): pl.pallas_call(finish, out_shape=tuple((jax.ShapeDtypeStruct(r.shape, r.d...]
    unnamed x7 -> x0, local copies, waits for them, and re-layouts: 3.13 us -> none
where the time goes in v4:
time: 168 us; the launch traced here: 167 us
  Pallas kernels  167 us (99%)
    pallas_call x1, Pallas kernels, body(): pl.pallas_call(kernel, out_shape=(jax.ShapeDtypeStruct((buckets, edges),...  149 us
    pallas_call x1, Pallas kernels, body(): pl.pallas_call(finish, out_shape=tuple((jax.ShapeDtypeStruct(r.shape, r.d...  18.1 us

profile of v4, /device:TPU:16, one launch (start us, length us, event | category | flops | bytes accessed | tf_op | source)
XLA Modules:
  0.0 167.4 jit_solution(8381355390478396586)
XLA Ops:
  0.6 148.7 %shard_map.94 = (f32[32,4096]{1,0:T(8,128)}, f32[32,256]{1,0:T(8,128)}, f32[3,2,32]{2,1,0:T(2,128)}) custom-call(f32[32,4096]{1,0:T(8,128)} %cost_ref.1, f32[32,4096]{1,0:T(8,128)} %bound_ref.1, f32[32,4096]{1,0:T(8,128)} %start_ref.1, f32[32,256]{1,0:T(8,128)} %dual_ref.1, f32[32,256]{1,0:T(8,128)} %target_ref.1, s32[2,4096]{1,0:T(2,128)} %bitcast.3, ...), custom_call_target="tpu_custom_call" | custom-call | flops 51999997952 | bytes 4194304 | tf_op jit(solution)/shard_map/pallas_call | solution.py:349
  149.3 18.1 %shard_map.95 = (f32[32,4096]{1,0:T(8,128)}, f32[32,256]{1,0:T(8,128)}, f32[3,2,32]{2,1,0:T(2,128)}) custom-call(f32[32,4096]{1,0:T(8,128)} %get-tuple-element.9.refs_0_, f32[32,256]{1,0:T(8,128)} %get-tuple-element.10.refs_1_, f32[3,2,32]{2,1,0:T(2,128)} %get-tuple-element.11.refs_2_), custom_call_target="tpu_custom_call" | custom-call | tf_op jit(solution)/shard_map/pallas_call | solution.py:402

commit v5 on v4

--- a/solution.py
+++ b/solution.py
@@ -28,15 +28,15 @@
 def kernel(cost_ref, bound_ref, start_ref, dual_ref, target_ref, owner_ref, local_ref,
            primal_ref, duals_ref, totals_ref,
            cost, bound, primal, owner, local, hot, own_half, ext, left, acc,
-           packed, state, gath, part, rsz, deg_part, deg_z, deg_x, step, tot, tot_z, tot_x, back,
+           packed, state, gath, part, rsz, deg_part, deg_z, deg_x, step, tot, tot_all, back,
            sem_pack, sem_own, sem_loc, sem_cost, sem_bound, sem_primal, sem_agz, sem_rsz,
-           sem_dz, sem_dx, sem_tz, sem_tx, sem_back, sem_dual):
+           sem_dz, sem_dx, sem_tot, sem_back, sem_dual):
     edges = cost_ref.shape[1]
     slots = ITERS * CHUNKS
     me = lax.axis_index("edge")
     my_x = lax.rem(me, X)
     my_z = lax.div(me, X)
-    lane = lax.broadcasted_iota(jnp.int32, (GROUP, LANES), 1)
+    kind = lax.broadcasted_iota(jnp.int32, (GROUP, LANES), 1) >> 5
     upper = lax.broadcasted_iota(jnp.int32, (GROUP, LANES), 0) < HALF
 
     def x_of(j):
@@ -70,11 +70,18 @@
 
     def agz(c):
         block = gath.at[c, my_z]
-        return [remote(block, block, sem_agz.at[c, 0, j], sem_agz.at[c, 1, j], at_z(j)) for j in FAR]
+        return [remote(block, block, sem_agz.at[c, 0], sem_agz.at[c, 1], at_z(j)) for j in FAR]
+
+    def agz_all(c):
+        blocks = gath.at[c, pl.ds(0, Z - 1)]
+        return [remote(blocks, blocks, sem_agz.at[c, 0], sem_agz.at[c, 1], at_z(1))]
 
     def to_z(c):
-        return [remote(part.at[c, lax.rem(my_z + j, Z)], rsz.at[c, j - 1], sem_rsz.at[c, 0, j], sem_rsz.at[c, 1, j],
-                       at_z(j)) for j in FAR]
+        return [remote(part.at[c, lax.rem(my_z + j, Z)], rsz.at[c, j - 1], sem_rsz.at[c, 0], sem_rsz.at[c, 1], at_z(j))
+                for j in FAR]
+
+    def to_z_all(c):
+        return [remote(part.at[c, pl.ds(0, Z - 1)], rsz.at[c], sem_rsz.at[c, 0], sem_rsz.at[c, 1], at_z(1))]
 
     def deg_to_z():
         return [remote(deg_part.at[lax.rem(my_z + j, Z)], deg_z.at[j - 1], sem_dz.at[0, j], sem_dz.at[1, j], at_z(j))
@@ -83,13 +90,13 @@
     def deg_to_x():
         return [give(deg_x.at[0], deg_x, sem_dx, j) for j in range(1, X)]
 
-    def tot_to_z():
-        return [remote(tot_z.at[my_z], tot_z.at[my_z], sem_tz.at[0, j], sem_tz.at[1, j], at_z(j))
-                for j in range(1, Z)]
-
-    def tot_to_x():
-        return [remote(tot_x.at[my_x], tot_x.at[my_x], sem_tx.at[0, j], sem_tx.at[1, X - j], at_x(j))
-                for j in range(1, X)]
+    def tot_out(j):
+        mine = tot_all.at[me]
+        return remote(mine, mine, sem_tot.at[0], sem_tot.at[1], lax.rem(me + j, OWNERS))
+
+    def tot_in():
+        rows = tot_all.at[pl.ds(0, OWNERS - 1)]
+        return remote(rows, rows, sem_tot.at[0], sem_tot.at[1], at_z(1))
 
     def primal_back(j):
         return remote(primal.at[j], primal_ref.at[group(my_x)], sem_back.at[0, j], sem_back.at[1, X - j], at_x(j))
@@ -106,18 +113,17 @@
             copy.wait()
 
     for g in range(X):
-        for kind, ref in enumerate((dual_ref, target_ref)):
+        for which, ref in enumerate((dual_ref, target_ref)):
             rows = ref[g * GROUP:(g + 1) * GROUP, :]
             low, high = rows[:, :LANES], rows[:, LANES:]
-            packed[g, 2 * kind] = jnp.concatenate([low[:HALF], high[:HALF]], axis=0)
-            packed[g, 2 * kind + 1] = jnp.concatenate([low[HALF:], high[HALF:]], axis=0)
+            packed[g, 2 * which] = jnp.concatenate([low[:HALF], high[:HALF]], axis=0)
+            packed[g, 2 * which + 1] = jnp.concatenate([low[HALF:], high[HALF:]], axis=0)
 
     barrier = pltpu.get_barrier_semaphore()
-    for j in range(1, Z):
-        pl.semaphore_signal(barrier, inc=1, device_id={"edge": at_z(j)}, device_id_type=pl.DeviceIdType.MESH)
-    for j in range(1, X):
-        pl.semaphore_signal(barrier, inc=1, device_id={"edge": at_x(j)}, device_id_type=pl.DeviceIdType.MESH)
-    pl.semaphore_wait(barrier, Z + X - 2)
+    for j in range(1, OWNERS):
+        pl.semaphore_signal(barrier, inc=1, device_id={"edge": lax.rem(me + j, OWNERS)},
+                            device_id_type=pl.DeviceIdType.MESH)
+    pl.semaphore_wait(barrier, OWNERS - 1)
 
     peers = (3, 1, 2)
 
@@ -204,7 +210,7 @@
 
     def settle(t):
         c, sweep = lax.rem(t, CHUNKS), lax.div(t, CHUNKS)
-        wait(to_z(c))
+        wait(to_z_all(c))
         squares = jnp.zeros((GROUP, LANES), F32)
         for x in range(X):
             place = lax.rem(x + X - my_x, X)
@@ -218,7 +224,7 @@
             squares = squares + residual * residual
         square = jnp.broadcast_to(jnp.sum(squares, axis=1, keepdims=True), (GROUP, LANES))
         square = square + turn(square)
-        tot[...] += jnp.where((lane == sweep) & (upper == (c == 0)), square, 0.0)
+        tot[0] += jnp.where((kind == sweep) & (upper == (c == 0)), square, 0.0)
 
         @pl.when(sweep < ITERS - 1)
         def _():
@@ -226,7 +232,7 @@
 
     def slot(t, carry):
         c, sweep = lax.rem(t, CHUNKS), lax.div(t, CHUNKS)
-        wait(agz(c))
+        wait(agz_all(c))
         value = gath[c].reshape(OWNERS, GROUP, LANES)
         high = value.astype(BF16).astype(F32)
         low = value - high
@@ -238,22 +244,17 @@
         in_chunk = (lax.broadcasted_iota(jnp.int32, (GROUP, edges), 0) >= HALF) == (c == 1)
         acc[...] = jnp.zeros_like(acc)
 
-        def block(i, spend):
-            j = jnp.where(i < 2, i, 5 - i)
+        def place(i):
+            return jnp.where(i < 2, i, 5 - i)
+
+        def pull(i, carry):
+            j = place(i)
 
             @pl.when((t == 0) & (i > 0))
             def _():
                 taken(cost, sem_cost, j).wait_recv()
                 taken(bound, sem_bound, j).wait_recv()
                 taken(primal, sem_primal, j).wait_recv()
-
-            @pl.when((t == 1) & (i == 2))
-            def _():
-                degree_done()
-
-            @pl.when((t >= 1) & (i == 2))
-            def _():
-                settle(t - 1)
 
             cols = pl.ds(pl.multiple_of(j * edges, edges), edges)
             ends = []
@@ -274,24 +275,45 @@
             high = extended.astype(BF16).astype(F32)
             both = jnp.where(in_upper, high, extended - high)
             both = jnp.concatenate([both, both], axis=0).astype(BF16)
-            ext[0] = both
-            ext[1] = -both
+            ext[0, :, cols] = both
+            ext[1, :, cols] = -both
+            spend = jnp.sum(jnp.where(in_chunk, price * moved, 0.0), axis=1, keepdims=True)
+            tot[1] += jnp.where(kind == sweep, jnp.broadcast_to(spend, (GROUP, LANES)), 0.0)
 
             @pl.when((t == slots - 1) & (i > 0))
             def _():
                 primal_back(j).start()
 
+            return carry
+
+        def push(i, carry):
+            j = place(i)
+            cols = pl.ds(pl.multiple_of(j * edges, edges), edges)
             for side in range(2):
-                value, names = ext[side], own_half[side, :, cols]
+                value, names = ext[side, :, cols], own_half[side, :, cols]
                 zero = jnp.zeros_like(value)
                 masked = jnp.concatenate(
                     [jnp.where(names == BF16(o), value, zero) for o in range(0, OWNERS, 2)], axis=0)
                 acc[...] += lax.dot_general(masked, hot[side, :, cols], (((1,), (1,)), ((), ())),
                                             preferred_element_type=F32)
-            return spend + jnp.sum(jnp.where(in_chunk, price * moved, 0.0), axis=1, keepdims=True)
-
-        spend = lax.fori_loop(0, X, block, jnp.zeros((GROUP, 1), F32))
-        tot[...] += jnp.where(lane == ITERS + sweep, jnp.broadcast_to(spend, (GROUP, LANES)), 0.0)
+            return carry
+
+        def turns(p, carry):
+            low, high = jnp.where(p == 0, 0, X - 1), jnp.where((t == 0) & (p == 0), X - 1, X)
+            lax.fori_loop(low, high, pull, 0)
+
+            @pl.when(t == 1)
+            def _():
+                degree_done()
+
+            @pl.when(t >= 1)
+            def _():
+                settle(t - 1)
+
+            lax.fori_loop(low, high, push, 0)
+            return carry
+
+        lax.fori_loop(0, jnp.where(t == 0, 2, 1), turns, 0)
         value = acc[...].reshape(OWNERS, GROUP, 2 * LANES)
         value = value + turn(value)
         part[c] = jnp.where(is_upper, value[:, :, :LANES], value[:, :, LANES:]).reshape(Z, X, GROUP, LANES)
@@ -301,8 +323,13 @@
     lax.fori_loop(0, slots, slot, 0)
     settle(slots - 1)
 
-    tot_z[my_z] = tot[...]
-    start(tot_to_z())
+    lane = lax.broadcasted_iota(jnp.int32, (GROUP, LANES), 1) & (X * GROUP - 1)
+    bucket = lax.broadcasted_iota(jnp.int32, (GROUP, LANES), 0) + my_x * GROUP
+    for side in range(2):
+        row = jnp.sum(jnp.where(lane == bucket, tot[side], 0.0), axis=0, keepdims=True)
+        tot_all[me, :, side * LANES:(side + 1) * LANES] = row
+    for j in range(1, OWNERS):
+        tot_out(j).start()
     for j in range(X):
         first, second = state[j, 0], state[j, 1]
         back[j] = jnp.concatenate(
@@ -315,29 +342,23 @@
     for j in peers:
         for copy in give_arrays(j):
             copy.wait_send()
-    wait(tot_to_z())
-    mine = tot_z[0]
-    for z in range(1, Z):
-        mine = mine + tot_z[z]
-    tot_x[my_x] = mine
-    start(tot_to_x())
     wait([primal_back(j) for j in peers])
     wait([dual_back(j) for j in peers])
-    wait(tot_to_x())
-    every = jnp.concatenate([tot_x[x] for x in range(X)] + [jnp.zeros((LANES - X * GROUP, LANES), F32)], axis=0).T
-    for i in range(ITERS):
-        totals_ref[i, 0:1, :] = every[i:i + 1, :X * GROUP]
-        totals_ref[i, 1:2, :] = every[ITERS + i:ITERS + i + 1, :X * GROUP]
+    tot_in().wait()
+    total = tot_all[0]
+    for other in range(1, OWNERS):
+        total = total + tot_all[other]
+    for side in range(2):
+        row = jnp.broadcast_to(total[:, side * LANES:(side + 1) * LANES], (GROUP, LANES))
+        for i in range(ITERS):
+            turned = pltpu.roll(row, (LANES - i * X * GROUP) % LANES, 1)
+            totals_ref[i, side:side + 1, :] = turned[:1, :X * GROUP]
 
 
 def finish(*refs):
     count = len(refs) // 2
-    sems = refs[-1]
-    copies = [pltpu.make_async_copy(refs[i], refs[count + i], sems.at[i]) for i in range(count)]
-    for copy in copies:
-        copy.start()
-    for copy in copies:
-        copy.wait()
+    for i in range(count):
+        refs[count + i][...] = refs[i][...]
 
 
 def body(unit_cost, upper_bound, start_primal, start_dual, net_target, owners, local_ids):
@@ -363,7 +384,7 @@
             vmem((X, 2, edges), jnp.int32),
             vmem((2, accounts, X * edges), BF16),
             vmem((2, 2 * GROUP, X * edges), BF16),
-            vmem((2, 2 * GROUP, edges), BF16),
+            vmem((2, 2 * GROUP, X * edges), BF16),
             vmem((OWNERS * GROUP, accounts), BF16),
             vmem((OWNERS * GROUP, accounts), F32),
             vmem((X, 2 * CHUNKS) + tile, F32),
@@ -375,9 +396,8 @@
             vmem((Z - 1, GROUP, accounts), F32),
             vmem((X, GROUP, accounts), F32),
             vmem((X,) + tile, F32),
-            vmem(tile, F32),
-            vmem((Z,) + tile, F32),
-            vmem((X,) + tile, F32),
+            vmem((2,) + tile, F32),
+            vmem((OWNERS, 1, 2 * LANES), F32),
             vmem((X, GROUP, accounts), F32),
             dma((2, X)),
             dma((2, X)),
@@ -385,12 +405,11 @@
             dma((2, X)),
             dma((2, X)),
             dma((2, X)),
-            dma((CHUNKS, 2, Z)),
-            dma((CHUNKS, 2, Z)),
+            dma((CHUNKS, 2)),
+            dma((CHUNKS, 2)),
             dma((2, Z)),
             dma((2, X)),
-            dma((2, Z)),
-            dma((2, X)),
+            dma((2,)),
             dma((2, X)),
             dma((2, X)),
         ],
@@ -402,9 +421,8 @@
     primal, duals, totals = pl.pallas_call(
         finish,
         out_shape=tuple(jax.ShapeDtypeStruct(r.shape, r.dtype) for r in results),
-        in_specs=[pl.BlockSpec(memory_space=pl.ANY)] * 3,
-        out_specs=[pl.BlockSpec(memory_space=pl.ANY)] * 3,
-        scratch_shapes=[dma((3,))],
+        in_specs=[pl.BlockSpec(memory_space=vmem)] * 3,
+        out_specs=[pl.BlockSpec(memory_space=vmem)] * 3,
         compiler_params=pltpu.CompilerParams(vmem_limit_bytes=60 * 2**20),
     )(*results)
     return primal, duals, totals.transpose(1, 0, 2)

time: 168 us -> 106 us (0.63)
  Pallas kernels: 167 us -> 105 us
    pallas_call x1, Pallas kernels: 149 us -> 103 us  [body(): pl.pallas_call(kernel, out_shape=(jax.ShapeDtypeStruct((buckets, edges),...]
    pallas_call x1, Pallas kernels: 18.1 us -> 1.9 us  [body(): pl.pallas_call(finish, out_shape=tuple((jax.ShapeDtypeStruct(r.shape, r.d...]
where the time goes in v5:
time: 106 us
  Pallas kernels  105 us (99%)
    pallas_call x1, Pallas kernels, body(): pl.pallas_call(kernel, out_shape=(jax.ShapeDtypeStruct((buckets, edges),...  103 us

profile of v5, /device:TPU:16, one launch (start us, length us, event | category | flops | bytes accessed | tf_op | source)
XLA Modules:
  0.0 105.6 jit_solution(5111772328466703011)
XLA Ops:
  0.6 103.0 %shard_map.94 = (f32[32,4096]{1,0:T(8,128)}, f32[32,256]{1,0:T(8,128)}, f32[3,2,32]{2,1,0:T(2,128)}) custom-call(f32[32,4096]{1,0:T(8,128)} %cost_ref.1, f32[32,4096]{1,0:T(8,128)} %bound_ref.1, f32[32,4096]{1,0:T(8,128)} %start_ref.1, f32[32,256]{1,0:T(8,128)} %dual_ref.1, f32[32,256]{1,0:T(8,128)} %target_ref.1, s32[2,4096]{1,0:T(2,128)} %bitcast.3, ...), custom_call_target="tpu_custom_call" | custom-call | flops 51999997952 | bytes 4194304 | tf_op jit(solution)/shard_map/pallas_call | solution.py:370
  103.7 1.9 %shard_map.95 = (f32[32,4096]{1,0:T(8,128)}, f32[32,256]{1,0:T(8,128)}, f32[3,2,32]{2,1,0:T(2,128)}) custom-call(f32[32,4096]{1,0:T(8,128)} %get-tuple-element.9.refs_0_, f32[32,256]{1,0:T(8,128)} %get-tuple-element.10.refs_1_, f32[3,2,32]{2,1,0:T(2,128)} %get-tuple-element.11.refs_2_), custom_call_target="tpu_custom_call" | custom-call | tf_op jit(solution)/shard_map/pallas_call | solution.py:421

commit v6 on v5

--- a/solution.py
+++ b/solution.py
@@ -30,7 +30,7 @@
            cost, bound, primal, owner, local, hot, own_half, ext, left, acc,
            packed, state, gath, part, rsz, deg_part, deg_z, deg_x, step, tot, tot_all, back,
            sem_pack, sem_own, sem_loc, sem_cost, sem_bound, sem_primal, sem_agz, sem_rsz,
-           sem_dz, sem_dx, sem_tot, sem_back, sem_dual):
+           sem_dz, sem_dx, sem_tot, sem_back, sem_dual, sem_here):
     edges = cost_ref.shape[1]
     slots = ITERS * CHUNKS
     me = lax.axis_index("edge")
@@ -119,6 +119,10 @@
             packed[g, 2 * which] = jnp.concatenate([low[:HALF], high[:HALF]], axis=0)
             packed[g, 2 * which + 1] = jnp.concatenate([low[HALF:], high[HALF:]], axis=0)
 
+    def own_rows():
+        return [pltpu.make_async_copy(src.at[group(my_x)], dst.at[0], sem_here.at[i])
+                for i, (src, dst) in enumerate(((cost_ref, cost), (bound_ref, bound), (start_ref, primal)))]
+
     barrier = pltpu.get_barrier_semaphore()
     for j in range(1, OWNERS):
         pl.semaphore_signal(barrier, inc=1, device_id={"edge": lax.rem(me + j, OWNERS)},
@@ -140,9 +144,7 @@
     state[0] = packed[my_x]
     owner[0] = owner_ref[...]
     local[0] = local_ref[...]
-    cost[0] = cost_ref[group(my_x), :]
-    bound[0] = bound_ref[group(my_x), :]
-    primal[0] = start_ref[group(my_x), :]
+    start(own_rows())
 
     def build(j):
         second = lax.broadcasted_iota(jnp.int32, (2 * GROUP, 256), 0) >= GROUP
@@ -192,12 +194,13 @@
 
     lax.fori_loop(1, X, later, 0)
 
-    wait(deg_to_z())
-    mine = deg_part[my_z]
-    for j in range(Z - 1):
-        mine = mine + deg_z[j]
-    deg_x[0] = mine
-    start(deg_to_x())
+    def degree_passed():
+        wait(deg_to_z())
+        mine = deg_part[my_z]
+        for j in range(Z - 1):
+            mine = mine + deg_z[j]
+        deg_x[0] = mine
+        start(deg_to_x())
 
     def degree_done():
         wait(deg_to_x())
@@ -318,8 +321,14 @@
         value = value + turn(value)
         part[c] = jnp.where(is_upper, value[:, :, :LANES], value[:, :, LANES:]).reshape(Z, X, GROUP, LANES)
         start(to_z(c))
+
+        @pl.when(t == 0)
+        def _():
+            degree_passed()
+
         return carry
 
+    wait(own_rows())
     lax.fori_loop(0, slots, slot, 0)
     settle(slots - 1)
 
@@ -374,7 +383,7 @@
             jax.ShapeDtypeStruct((buckets, accounts), F32),
             jax.ShapeDtypeStruct((ITERS, 2, buckets), F32),
         ),
-        in_specs=[pl.BlockSpec(memory_space=vmem)] * 7,
+        in_specs=[pl.BlockSpec(memory_space=pl.ANY)] * 3 + [pl.BlockSpec(memory_space=vmem)] * 4,
         out_specs=[pl.BlockSpec(memory_space=vmem)] * 3,
         scratch_shapes=[
             vmem((X, GROUP, edges), F32),
@@ -412,6 +421,7 @@
             dma((2,)),
             dma((2, X)),
             dma((2, X)),
+            dma((3,)),
         ],
         compiler_params=pltpu.CompilerParams(
             collective_id=0, has_side_effects=True, vmem_limit_bytes=58 * 2**20),

time: 106 us -> 105 us (level)
  no operation moved by 1% of the time
where the time goes in v6:
time: 105 us
  Pallas kernels  104 us (99%)
    pallas_call x1, Pallas kernels, body(): pl.pallas_call(kernel, out_shape=(jax.ShapeDtypeStruct((buckets, edges),...  102 us

profile of v6, /device:TPU:16, one launch (start us, length us, event | category | flops | bytes accessed | tf_op | source)
XLA Modules:
  0.0 104.9 jit_solution(2642583382486300651)
XLA Ops:
  0.6 102.3 %shard_map.94 = (f32[32,4096]{1,0:T(8,128)}, f32[32,256]{1,0:T(8,128)}, f32[3,2,32]{2,1,0:T(2,128)}) custom-call(f32[32,4096]{1,0:T(8,128)} %cost_ref.1, f32[32,4096]{1,0:T(8,128)} %bound_ref.1, f32[32,4096]{1,0:T(8,128)} %start_ref.1, f32[32,256]{1,0:T(8,128)} %dual_ref.1, f32[32,256]{1,0:T(8,128)} %target_ref.1, s32[2,4096]{1,0:T(2,128)} %bitcast.3, ...), custom_call_target="tpu_custom_call" | custom-call | flops 51999997952 | bytes 4194304 | tf_op jit(solution)/shard_map/pallas_call | solution.py:379
  103.0 1.9 %shard_map.95 = (f32[32,4096]{1,0:T(8,128)}, f32[32,256]{1,0:T(8,128)}, f32[3,2,32]{2,1,0:T(2,128)}) custom-call(f32[32,4096]{1,0:T(8,128)} %get-tuple-element.9.refs_0_, f32[32,256]{1,0:T(8,128)} %get-tuple-element.10.refs_1_, f32[3,2,32]{2,1,0:T(2,128)} %get-tuple-element.11.refs_2_), custom_call_target="tpu_custom_call" | custom-call | tf_op jit(solution)/shard_map/pallas_call | solution.py:431

commit v7 on v6

--- a/solution.py
+++ b/solution.py
@@ -167,7 +167,7 @@
     for c in range(CHUNKS):
         for x in range(X):
             gath[c, my_z, x] = state[lax.rem(x + X - my_x, X), c]
-        start(agz(c))
+    start(agz(0))
     start(give_arrays(3) + give_arrays(1))
     build(0)
 
@@ -180,7 +180,6 @@
     for z in range(Z):
         four = degree[z * X:(z + 1) * X]
         deg_part[z] = jnp.concatenate([four, four], axis=0)
-    start(deg_to_z())
     tot[...] = jnp.zeros_like(tot)
 
     for j in peers:
@@ -193,6 +192,8 @@
         return carry
 
     lax.fori_loop(1, X, later, 0)
+    start(agz(1))
+    start(deg_to_z())
 
     def degree_passed():
         wait(deg_to_z())

time: 105 us -> 105 us (level)
  no operation moved by 1% of the time
where the time goes in v7:
time: 105 us
  Pallas kernels  104 us (99%)
    pallas_call x1, Pallas kernels, body(): pl.pallas_call(kernel, out_shape=(jax.ShapeDtypeStruct((buckets, edges),...  102 us

profile of v7, /device:TPU:16, one launch (start us, length us, event | category | flops | bytes accessed | tf_op | source)
XLA Modules:
  0.0 104.9 jit_solution(809153112406206540)
XLA Ops:
  0.6 102.3 %shard_map.94 = (f32[32,4096]{1,0:T(8,128)}, f32[32,256]{1,0:T(8,128)}, f32[3,2,32]{2,1,0:T(2,128)}) custom-call(f32[32,4096]{1,0:T(8,128)} %cost_ref.1, f32[32,4096]{1,0:T(8,128)} %bound_ref.1, f32[32,4096]{1,0:T(8,128)} %start_ref.1, f32[32,256]{1,0:T(8,128)} %dual_ref.1, f32[32,256]{1,0:T(8,128)} %target_ref.1, s32[2,4096]{1,0:T(2,128)} %bitcast.3, ...), custom_call_target="tpu_custom_call" | custom-call | flops 51999997952 | bytes 4194304 | tf_op jit(solution)/shard_map/pallas_call | solution.py:380
  103.0 1.9 %shard_map.95 = (f32[32,4096]{1,0:T(8,128)}, f32[32,256]{1,0:T(8,128)}, f32[3,2,32]{2,1,0:T(2,128)}) custom-call(f32[32,4096]{1,0:T(8,128)} %get-tuple-element.9.refs_0_, f32[32,256]{1,0:T(8,128)} %get-tuple-element.10.refs_1_, f32[3,2,32]{2,1,0:T(2,128)} %get-tuple-element.11.refs_2_), custom_call_target="tpu_custom_call" | custom-call | tf_op jit(solution)/shard_map/pallas_call | solution.py:432
